TPU v7x, 512 devices: a whole 4x4x16 slice. The times are simulated.
512 devices in a mesh: corpus: 128 (over y, z, core), query: 4 (over x).
Axes of the slice: x: 4, y: 4, z: 16, core: 2. Of those that a mesh axis runs over, the one named last changes fastest.
Arguments:
- queries_in: bfloat16 [512, 768], P('query'), may hold values from -6 to 6
- head_weight: bfloat16 [768, 768], replicated, may hold values from -0.21875 to 0.21875
- codebook: bfloat16 [96, 2048], replicated, may hold values from -40 to 40
- codes: int32 [49152, 96], P('corpus'), may hold values from 0 to 255
- slab_sizes: int32 [128], P('corpus'), may hold values from 1 to 384, as said below
- positive_ids: int32 [512], P('query'), may hold values from 0 to 49151, as said below
Outputs:
- query_loss: float32 [512], P('query')
- head_grad: float32 [768, 768], P('query')
- codebook_grad: float32 [96, 2048], replicated
Inputs may be any that keep to these rules, and one draw needn't show every extreme that they name: `slab_sizes`: live passages of each slab of 384 slots; one shard's slab is full and another holds one passage. `positive_ids`: each names a live slot, counting the slabs of the corpus shards one after another.
All inputs are finite; a program needn't handle non-finite values.
Results may differ from a plain program's by a relative error of at most 0.0045.
Values may be sent and summed in bfloat16 or wider, within the bound.
A program may use at most 64 MiB of HBM per device.

v0:
```python
import jax
import jax.numpy as jnp
from jax import lax
from jax.sharding import PartitionSpec as P

D = 768
M = 96
K = 256
SUB = 8
GROUP = 16
BLOCK = 512
SLOT_DEV = 384


def rebuild(code_rows, centroids):
    row_count = code_rows.shape[0]
    pieces = []
    for first_sub in range(0, M, GROUP):
        chosen = code_rows[:, first_sub : first_sub + GROUP]
        onehot = (chosen[:, :, None] == jnp.arange(K, dtype=jnp.int32)[None, None, :]).astype(
            jnp.bfloat16
        )
        block_part = jnp.einsum(
            "rgk,gks->rgs",
            onehot,
            centroids[first_sub : first_sub + GROUP],
            preferred_element_type=jnp.float32,
        )
        pieces.append(block_part.reshape(row_count, GROUP * SUB))
    return jnp.concatenate(pieces, axis=1).astype(jnp.bfloat16)


def book_terms(code_rows, block_grads):
    row_count = code_rows.shape[0]
    shaped = block_grads.reshape(row_count, M, SUB)
    upper = shaped.astype(jnp.bfloat16)
    lower = (shaped - upper.astype(jnp.float32)).astype(jnp.bfloat16)
    pieces = []
    for first_sub in range(0, M, GROUP):
        chosen = code_rows[:, first_sub : first_sub + GROUP]
        onehot = (chosen[:, :, None] == jnp.arange(K, dtype=jnp.int32)[None, None, :]).astype(
            jnp.bfloat16
        )
        high_part = jnp.einsum(
            "rgs,rgk->gsk",
            upper[:, first_sub : first_sub + GROUP],
            onehot,
            preferred_element_type=jnp.float32,
        )
        low_part = jnp.einsum(
            "rgs,rgk->gsk",
            lower[:, first_sub : first_sub + GROUP],
            onehot,
            preferred_element_type=jnp.float32,
        )
        pieces.append(high_part + low_part)
    return jnp.transpose(jnp.concatenate(pieces, axis=0), (0, 2, 1))


def shards(queries_in, head_weight, codebook, codes, slab_sizes, positive_ids):
    query_vec = jnp.dot(queries_in, head_weight, preferred_element_type=jnp.float32).astype(
        jnp.bfloat16
    )
    centroids = codebook.reshape(M, K, SUB)
    length = slab_sizes[0]
    owner_index = lax.axis_index("corpus")
    padded = (SLOT_DEV + BLOCK - 1) // BLOCK * BLOCK
    code_pad = jnp.pad(codes, ((0, padded - SLOT_DEV), (0, 0)))
    row_offsets = jnp.arange(BLOCK, dtype=jnp.int32)

    def build_block(block_step, stored):
        block_start = block_step * BLOCK
        block_rows = rebuild(code_pad, centroids)
        block_rows = jnp.where(
            (block_start + row_offsets < length)[:, None], block_rows, jnp.zeros_like(block_rows)
        )
        return lax.dynamic_update_slice_in_dim(stored, block_rows, block_start, 0)

    own_blocks = (length + BLOCK - 1) // BLOCK
    passages = lax.fori_loop(0, own_blocks, build_block, jnp.zeros((padded, D), jnp.bfloat16))
    local_slot = positive_ids - owner_index * SLOT_DEV
    owned_mask = (local_slot >= 0) & (local_slot < SLOT_DEV)
    pos_codes = codes[jnp.clip(local_slot, 0, SLOT_DEV - 1)]
    pos_rows = rebuild(pos_codes, centroids)
    pos_rows = jnp.where(owned_mask[:, None], pos_rows, jnp.zeros_like(pos_rows))
    pos_score = jnp.sum(query_vec.astype(jnp.float32) * pos_rows.astype(jnp.float32), axis=1)
    live_blocks = (length + BLOCK - 1) // BLOCK

    def score_block(block_step, stored):
        block_start = block_step * BLOCK
        block_part = lax.dot_general(
            query_vec, passages, (((1,), (1,)), ((), ())), preferred_element_type=jnp.float32
        )
        block_part = jnp.where((block_start + row_offsets < length)[None, :], block_part, -jnp.inf)
        return block_part

    query_count = queries_in.shape[0]
    scores = lax.fori_loop(
        0, live_blocks, score_block, jnp.full((query_count, padded), -jnp.inf, jnp.float32)
    )
    local_peak = jnp.max(scores, axis=1)
    row_peak = lax.pmax(local_peak, "corpus")
    local_total = jnp.sum(jnp.exp(scores - row_peak[:, None]), axis=1)
    totals, pos_total = lax.psum((local_total, pos_score), "corpus")
    log_total = row_peak + jnp.log(totals)
    query_loss = log_total - pos_total

    def descend(block_step, loop_state):
        query_grad, passage_grad = loop_state
        block_start = block_step * BLOCK
        soft_probs = jnp.exp(scores - log_total[:, None]).astype(jnp.bfloat16)
        query_grad = query_grad + jnp.dot(soft_probs, passages, preferred_element_type=jnp.float32)
        block_grads = lax.dot_general(
            soft_probs, query_vec, (((0,), (0,)), ((), ())), preferred_element_type=jnp.float32
        )
        passage_grad = block_grads
        return (query_grad, passage_grad)

    start_grads = (jnp.zeros((query_count, D), jnp.float32), jnp.zeros((padded, D), jnp.float32))
    query_grad, passage_grad = lax.fori_loop(0, live_blocks, descend, start_grads)
    query_grad = query_grad - pos_rows.astype(jnp.float32)

    def accumulate(block_step, book_grad):
        block_start = block_step * BLOCK
        block_grads = passage_grad
        block_grads = jnp.where(
            (block_start + row_offsets < length)[:, None], block_grads, jnp.zeros_like(block_grads)
        )
        return book_grad + book_terms(code_pad, block_grads)

    book_grad = lax.fori_loop(0, own_blocks, accumulate, jnp.zeros((M, K, SUB), jnp.float32))
    pos_queries = jnp.where(
        owned_mask[:, None], query_vec.astype(jnp.float32), jnp.zeros((query_count, D), jnp.float32)
    )
    book_grad = book_grad - book_terms(pos_codes, pos_queries)
    flat_book = book_grad.reshape(M, K * SUB)
    query_grad = lax.psum(query_grad, "corpus")
    flat_book = lax.psum(flat_book, ("corpus", "query"))
    grad_rounded = query_grad.astype(jnp.bfloat16)
    head_grad = lax.psum_scatter(
        lax.dot_general(
            queries_in, grad_rounded, (((0,), (0,)), ((), ())), preferred_element_type=jnp.float32
        ),
        "query",
        scatter_dimension=0,
        tiled=True,
    )
    return (query_loss, head_grad, flat_book)


def solution(mesh):
    return jax.shard_map(
        shards,
        mesh=mesh,
        in_specs=(P("query", None), P(), P(), P("corpus", None), P("corpus"), P("query")),
        out_specs=(P("query"), P("query", None), P()),
        check_vma=False,
    )
```

profile of v0, /device:TPU:1, one launch (start us, length us, event | category | flops | bytes accessed | tf_op | source)
XLA Modules:
  0.0 1122.5 jit_solution(12574151733020547526)
XLA Ops:
  10.2 1.0 copy.92
  11.2 1.6 pad.4
  16.2 2.0 fusion.89
  19.6 2.0 fusion.87
  23.0 2.0 fusion.86
  26.4 2.0 fusion.85
  29.8 2.0 fusion.84
  33.2 2.0 fusion.88
  36.5 1.7 while.54
  37.2 1.0 broadcast_select_fusion.5
  38.6 1.6 fusion.141
  40.9 1.4 while.55
  42.3 1.1 reduce_max.9
  43.4 254.7 %pmax.7 = f32[128]{0:T(128)S(1)} all-reduce(f32[128]{0:T(128)S(1)} %reduce_max.9), channel_id=1, replica_groups=mesh['corpus'=128,'query'=4] {'corpus'}, use_global_device_ids=true, to_apply=%region_5.6 | all-reduce | flops 128 | bytes 1024 | tf_op jit(solution)/shard_map/pmax | solution.py:102
  298.1 1.1 exponential_reduce_fusion
  299.2 251.2 %psum.28 = f32[128]{0:T(128)S(1)} all-reduce(f32[128]{0:T(128)S(1)} %exponential_reduce_fusion), channel_id=1, replica_groups=mesh['corpus'=128,'query'=4] {'corpus'}, use_global_device_ids=true, to_apply=%region_7.8 | all-reduce | flops 128 | bytes 1024 | tf_op jit(solution)/shard_map/psum | solution.py:104
  550.4 1.3 fusion.135
  551.7 1.3 broadcast.94
  553.0 1.7 while.53
  553.1 1.6 fusion.217
  556.6 1.1 fusion.60
  557.8 1.2 fusion.63
  558.9 1.1 fusion.66
  560.1 1.1 fusion.69
  561.2 1.2 fusion.72
  562.4 1.1 fusion.75
  563.5 1.9 copy.111
  565.4 19.7 %while.56 = (s32[]{:T(128)}, f32[96,256,8]{1,2,0:T(8,128)S(1)}, s32[]{:T(128)}, s32[]{:T(128)}, f32[512,768]{0,1:T(8,128)S(1)}, /*index=5*/s32[512,96]{0,1:T(8,128)}, s32[]{:T(128)}, s32[]{:T(128)}) while((s32[]{:T(128)}, f32[96,256,8]{1,2,0:T(8,128)S(1)}, s32[]{:T(128)}, s32[]{:T(128)}, f32[512,768]{0,1:T(8,128)S(1)}, ...), condition=%wide.region_15.16_spmd.clone, body=%wide.region_14.15_spmd.clone.sunk | while | flops 430179328 | bytes 18089064 | solution.py:131
  567.2 1.5 fusion.244
  568.7 1.5 fusion.242
  570.1 1.5 fusion.240
  571.6 1.5 fusion.238
  573.1 1.5 fusion.236
  574.5 1.5 fusion.234
  576.0 1.5 fusion.235
  577.5 1.5 fusion.237
  578.9 1.5 fusion.239
  580.4 1.5 fusion.241
  581.9 1.5 fusion.243
  583.3 1.5 fusion.245
  585.3 1.5 fusion.91
  586.8 1.5 fusion.93
  590.4 1.4 copy.113
  591.9 486.7 %all-reduce.6 = (f32[128]{0:T(128)S(1)}, bf16[128,768]{1,0:T(8,128)(2,1)}) all-reduce(f32[128]{0:T(128)S(1)} %get-tuple-element.517, f32[128,768]{1,0:T(8,128)S(1)} %copy-done.3), channel_id=1, replica_groups=mesh['corpus'=128,'query'=4] {'corpus'}, use_global_device_ids=true, to_apply=%region_9.10 | all-reduce | flops 98432 | bytes 590848 | tf_op jit(solution)/shard_map/psum | solution.py:104
  1078.6 1.5 convolution_bitcast_fusion
  1080.1 2.0 copy.116
  1082.6 2.4 copy.115
  1085.0 30.0 %reduce-scatter.4.cloned.1.call-done = f32[192,768]{1,0:T(8,128)} async-done(((f32[768,768]{1,0:T(8,128)}), f32[192,768]{1,0:T(8,128)}) %reduce-scatter.4.cloned.1.call-update) | async-done | bytes 589840
  (121 shorter events, 22.6 us)
Async XLA Ops:
  8.0 30.2 %copy-start = (bf16[768,768]{1,0:T(8,128)(2,1)S(1)}, bf16[768,768]{1,0:T(8,128)(2,1)}, u32[]{:S(2)}) copy-start(bf16[768,768]{1,0:T(8,128)(2,1)} %param.15) | copy-start | bytes 3538948
  8.0 6.9 copy-start.5
  8.0 1074.6 %all-reduce.5.cloned.1.call-start = ((), (), s32[]{:S(2)}) async-start(), calls=%async_computation.1 | async-start | bytes 2097152 | tf_op jit(solution)/shard_map/psum | solution.py:138
  14.6 543.2 %copy-start.7 = (s32[128,16]{0,1:T(8,128)}, s32[128,16]{0,1:T(8,128)S(1)}, u32[]{:S(2)}) copy-start(s32[128,16]{0,1:T(8,128)S(1)} %copy.101) | copy-start | bytes 24580
  14.7 544.2 %copy-start.9 = (s32[128,16]{0,1:T(8,128)}, s32[128,16]{0,1:T(8,128)S(1)}, u32[]{:S(2)}) copy-start(s32[128,16]{0,1:T(8,128)S(1)} %copy.99) | copy-start | bytes 24580
  14.7 545.3 %copy-start.11 = (s32[128,16]{0,1:T(8,128)}, s32[128,16]{0,1:T(8,128)S(1)}, u32[]{:S(2)}) copy-start(s32[128,16]{0,1:T(8,128)S(1)} %copy.97) | copy-start | bytes 24580
  14.8 546.4 %copy-start.13 = (s32[128,16]{0,1:T(8,128)}, s32[128,16]{0,1:T(8,128)S(1)}, u32[]{:S(2)}) copy-start(s32[128,16]{0,1:T(8,128)S(1)} %copy.95) | copy-start | bytes 24580
  14.9 547.5 %copy-start.14 = (s32[128,16]{0,1:T(8,128)}, s32[128,16]{0,1:T(8,128)S(1)}, u32[]{:S(2)}) copy-start(s32[128,16]{0,1:T(8,128)S(1)} %copy.93) | copy-start | bytes 24580
  36.5 1.7 copy-start.4
  38.6 511.9 %copy-start.2 = (bf16[512,768]{1,0:T(8,128)(2,1)S(1)}, bf16[512,768]{1,0:T(8,128)(2,1)}, u32[]{:S(2)}) copy-start(bf16[512,768]{1,0:T(8,128)(2,1)} %get-tuple-element.379) | copy-start | bytes 2359300
  42.3 510.7 %copy-start.1 = (f32[128,512]{1,0:T(8,128)S(1)}, f32[128,512]{1,0:T(8,128)}, u32[]{:S(2)}) copy-start(f32[128,512]{1,0:T(8,128)} %get-tuple-element.741) | copy-start | bytes 786436
  585.2 3.1 copy-start.6
  585.2 3.1 copy-start.12
  585.2 3.1 copy-start.18
  585.2 3.6 copy-start.10
  585.2 3.6 copy-start.17
  585.2 4.1 copy-start.8
  585.2 4.1 copy-start.16
  586.8 3.0 copy-start.15
  590.3 1.6 copy-start.3
  591.8 523.2 %reduce-scatter.4.cloned.1.call-start = ((), (), s32[]{:S(2)}) async-start(), calls=%async_computation.2 | async-start | bytes 2949120
Sparse Core Ops, SparseCore 0:
  592.0 455.8 all-reduce.4
Sparse Core Ops, SparseCore 1:
  1082.2 32.8 reduce-scatter.3
where the time goes:
time: 1120 us
  blocking collectives  993 us (89%)
  matrix products  50.7 us (5%)
  waiting for transfers between devices  30.1 us (3%)
  local copies, waits for them, and re-layouts  22 us (2%)
  between operations  16.8 us (2%)
    psum x2, blocking collectives, shards(): totals, pos_total = lax.psum((local_total, pos_score), 'corpus')  738 us
    pmax x1, blocking collectives, shards(): row_peak = lax.pmax(local_peak, 'corpus')  255 us
    unnamed x3, waiting for transfers between devices  30.1 us
  transfers between devices with their start and end apart: 2, of which 1 were waited for; matrix products, arithmetic and copies ran while one was open for 1% of the time, Pallas kernels for 0%

commit v1 on v0

v1 whole, which is shorter than its diff:
```python
import functools

import jax
import jax.numpy as jnp
from jax import lax
from jax.experimental import pallas as pl
from jax.experimental.pallas import tpu as pltpu
from jax.sharding import PartitionSpec as P

D = 768
M = 96
K = 256
SUB = 8
SLOT_DEV = 384
Q_DEV = 128
LANES = 128
TILES = 6
MESH = pl.DeviceIdType.MESH
NT = (((1,), (1,)), ((), ()))
VMEM_BYTES = 48 * 1024 * 1024


def grid_of(mesh):
    corpus, across = mesh.shape["corpus"], mesh.shape["query"]
    up = {128: 4, 8: 2}[corpus]
    return across, up, corpus // (2 * up)


def place(nz):
    c = lax.axis_index("corpus")
    return lax.axis_index("query"), c // (2 * nz), lax.rem(c // 2, nz), lax.rem(c, 2)


def score_kernel(
    length_ref, qin_ref, weight_ref, cent_ref, codes_ref, ids_ref,
    qt_ref, qint_ref, pt_ref, st_ref, codest_ref, stats_ref,
    codes_i, table_rows,
):
    query = jnp.dot(qin_ref[...], weight_ref[...], preferred_element_type=jnp.float32)
    query = query.astype(jnp.bfloat16)
    qt_ref[...] = query.astype(jnp.float32).T.astype(jnp.bfloat16)
    qint_ref[...] = qin_ref[...].astype(jnp.float32).T.astype(jnp.bfloat16)

    codes = codes_ref[...].astype(jnp.float32)
    codes = jnp.concatenate([codes, jnp.zeros((SLOT_DEV, LANES - M), jnp.float32)], axis=1)
    codes = codes.T
    codest_ref[...] = codes
    codes_i[...] = codes.astype(jnp.int32)

    def rebuild(pair, carry):
        halves = []
        for half in range(2):
            m = pair * 2 + half
            table = cent_ref[pl.ds(pl.multiple_of(m * SUB, SUB), SUB), :]
            row = codes_i[pl.ds(m, 1), :]
            parts = []
            for tile in range(SLOT_DEV // LANES):
                index = jnp.broadcast_to(row[:, tile * LANES : (tile + 1) * LANES], (SUB, LANES))
                low = index & (LANES - 1)
                first = jnp.take_along_axis(table[:, :LANES], low, axis=1, mode="promise_in_bounds")
                second = jnp.take_along_axis(table[:, LANES:], low, axis=1, mode="promise_in_bounds")
                parts.append(jnp.where(index >= LANES, second, first))
            halves.append(jnp.concatenate(parts, axis=1))
        rows = jnp.concatenate(halves, axis=0).astype(jnp.bfloat16)
        pt_ref[pl.ds(pl.multiple_of(pair * 2 * SUB, 2 * SUB), 2 * SUB), :] = rows
        return carry

    lax.fori_loop(0, M // 2, rebuild, 0, unroll=4)
    scores = jnp.dot(query, pt_ref[...], preferred_element_type=jnp.float32).T
    slot = lax.broadcasted_iota(jnp.int32, (SLOT_DEV, Q_DEV), 0)
    scores = jnp.where(slot < length_ref[0], scores, -jnp.inf)
    st_ref[...] = scores
    owned = slot == ids_ref[...] - lax.axis_index("corpus") * SLOT_DEV
    peak = jnp.max(scores, axis=0, keepdims=True)
    total = jnp.sum(jnp.exp(scores - peak), axis=0, keepdims=True)
    positive = jnp.sum(jnp.where(owned, scores, 0.0), axis=0, keepdims=True)
    stats_ref[0:1, :] = peak
    stats_ref[1:2, :] = total
    stats_ref[2:3, :] = positive
    stats_ref[3:8, :] = jnp.zeros((5, Q_DEV), jnp.float32)


def local_scores(length, queries_in, head_weight, cent, codes, ids):
    whole = pl.BlockSpec(memory_space=pltpu.VMEM)
    return pl.pallas_call(
        score_kernel,
        out_shape=[
            jax.ShapeDtypeStruct((D, Q_DEV), jnp.bfloat16),
            jax.ShapeDtypeStruct((D, Q_DEV), jnp.bfloat16),
            jax.ShapeDtypeStruct((D, SLOT_DEV), jnp.bfloat16),
            jax.ShapeDtypeStruct((SLOT_DEV, Q_DEV), jnp.float32),
            jax.ShapeDtypeStruct((LANES, SLOT_DEV), jnp.float32),
            jax.ShapeDtypeStruct((8, Q_DEV), jnp.float32),
        ],
        in_specs=[pl.BlockSpec(memory_space=pltpu.SMEM)] + [whole] * 5,
        out_specs=[whole] * 6,
        scratch_shapes=[
            pltpu.VMEM((LANES, SLOT_DEV), jnp.int32),
            pltpu.VMEM((8, LANES), jnp.float32),
        ],
        compiler_params=pltpu.CompilerParams(vmem_limit_bytes=VMEM_BYTES),
    )(length, queries_in, head_weight, cent, codes, ids)


def merge(slots):
    peaks, totals, positives = slots[:, 0, :], slots[:, 1, :], slots[:, 2, :]
    peak = jnp.max(peaks, axis=0, keepdims=True)
    total = jnp.sum(totals * jnp.exp(peaks - peak), axis=0, keepdims=True)
    return peak, total, jnp.sum(positives, axis=0, keepdims=True)


def totals_kernel(ny, nz, stats_ref, out_ref, near, far, mid, ns, nr, fs, fr):
    x, y, z, core = place(nz)
    group = ny * 2
    me = y * 2 + core

    def near_id(other):
        return {"corpus": ((other // 2) * nz + z) * 2 + lax.rem(other, 2), "query": x}

    def far_id(other):
        return {"corpus": (y * nz + other) * 2 + core, "query": x}

    barrier = pltpu.get_barrier_semaphore()

    def greet_near(d, carry):
        pl.semaphore_signal(barrier, 1, device_id=near_id(lax.rem(me + d, group)), device_id_type=MESH)
        return carry

    def greet_far(d, carry):
        pl.semaphore_signal(barrier, 1, device_id=far_id(lax.rem(z + d, nz)), device_id_type=MESH)
        return carry

    lax.fori_loop(1, group, greet_near, 0)
    lax.fori_loop(1, nz, greet_far, 0)
    pl.semaphore_wait(barrier, group + nz - 2)

    def near_copy(d):
        return pltpu.make_async_remote_copy(
            src_ref=stats_ref, dst_ref=near.at[me], send_sem=ns.at[d], recv_sem=nr.at[d],
            device_id=near_id(lax.rem(me + d, group)), device_id_type=MESH,
        )

    def far_copy(d):
        return pltpu.make_async_remote_copy(
            src_ref=mid, dst_ref=far.at[z], send_sem=fs.at[d], recv_sem=fr.at[d],
            device_id=far_id(lax.rem(z + d, nz)), device_id_type=MESH,
        )

    def loop(count, act):
        def body(d, carry):
            act(d)
            return carry

        lax.fori_loop(1, count, body, 0)

    loop(group, lambda d: near_copy(d).start())
    near[me] = stats_ref[...]
    loop(group, lambda d: near_copy(d).wait_recv())
    peak, total, positive = merge(near[...])
    pad = jnp.zeros((5, Q_DEV), jnp.float32)
    mid[...] = jnp.concatenate([peak, total, positive, pad], axis=0)
    loop(nz, lambda d: far_copy(d).start())
    far[z] = mid[...]
    loop(nz, lambda d: far_copy(d).wait_recv())
    peak, total, positive = merge(far[...])
    log_total = peak + jnp.log(total)
    out_ref[...] = jnp.concatenate([log_total, log_total - positive, positive, pad], axis=0)
    loop(group, lambda d: near_copy(d).wait_send())
    loop(nz, lambda d: far_copy(d).wait_send())


def query_totals(ny, nz, stats):
    whole = pl.BlockSpec(memory_space=pltpu.VMEM)
    dma = pltpu.SemaphoreType.DMA
    return pl.pallas_call(
        functools.partial(totals_kernel, ny, nz),
        out_shape=jax.ShapeDtypeStruct((8, Q_DEV), jnp.float32),
        in_specs=[whole],
        out_specs=whole,
        scratch_shapes=[
            pltpu.VMEM((ny * 2, 8, Q_DEV), jnp.float32),
            pltpu.VMEM((nz, 8, Q_DEV), jnp.float32),
            pltpu.VMEM((8, Q_DEV), jnp.float32),
            dma((ny * 2,)),
            dma((ny * 2,)),
            dma((nz,)),
            dma((nz,)),
        ],
        compiler_params=pltpu.CompilerParams(collective_id=0, has_side_effects=True),
    )(stats)


def grad_kernel(ids_ref, totals_ref, qt_ref, pt_ref, st_ref, codest_ref, grad_ref, book_ref, pgt):
    probs = jnp.exp(st_ref[...] - totals_ref[0:1, :]).astype(jnp.bfloat16)
    slot = lax.broadcasted_iota(jnp.int32, (SLOT_DEV, Q_DEV), 0)
    owned = slot == ids_ref[...] - lax.axis_index("corpus") * SLOT_DEV
    positive = jnp.where(owned, -1.0, 0.0).astype(jnp.bfloat16)
    both = jnp.concatenate([probs, positive], axis=1)
    query = qt_ref[...]
    pgt[...] = lax.dot_general(
        jnp.concatenate([query, query], axis=1), both, NT, preferred_element_type=jnp.float32
    )
    grads = jnp.dot(pt_ref[...], both, preferred_element_type=jnp.float32)
    grad_ref[...] = grads[:, :Q_DEV] + grads[:, Q_DEV:]
    word = lax.broadcasted_iota(jnp.int32, (K, SLOT_DEV), 0).astype(jnp.float32)
    word = word.astype(jnp.bfloat16)

    def scatter(m, carry):
        rows = pl.ds(pl.multiple_of(m * SUB, SUB), SUB)
        grad = pgt[rows, :]
        upper = grad.astype(jnp.bfloat16)
        lower = (grad - upper.astype(jnp.float32)).astype(jnp.bfloat16)
        code = codest_ref[pl.ds(m, 1), :].astype(jnp.bfloat16)
        onehot = jnp.where(word == code, jnp.bfloat16(1), jnp.bfloat16(0))
        halves = lax.dot_general(
            jnp.concatenate([upper, lower], axis=0), onehot, NT, preferred_element_type=jnp.float32
        )
        book_ref[rows, :] = halves[:SUB] + halves[SUB:]
        return carry

    lax.fori_loop(0, M, scatter, 0, unroll=8)


def local_grads(ids, totals, qt, pt, st, codest):
    whole = pl.BlockSpec(memory_space=pltpu.VMEM)
    return pl.pallas_call(
        grad_kernel,
        out_shape=[
            jax.ShapeDtypeStruct((D, Q_DEV), jnp.float32),
            jax.ShapeDtypeStruct((D, K), jnp.float32),
        ],
        in_specs=[whole] * 6,
        out_specs=[whole] * 2,
        scratch_shapes=[pltpu.VMEM((D, SLOT_DEV), jnp.float32)],
        compiler_params=pltpu.CompilerParams(vmem_limit_bytes=VMEM_BYTES),
    )(ids, totals, qt, pt, st, codest)


def sums_kernel(
    nx, ny, nz, grad_ref, book_ref, qint_ref, head_ref, out_ref,
    q_all, g_core, g_send, g_block, g_sum, g_z, g_red, g_fin,
    c_core, c_send, c_block, c_sum, c_z, c_red, c_fin,
    q_sems, gc_sems, gy_sems, gz_send, gz_recv, gr_send, gr_recv, gf_sems, gs_sems,
    cc_sems, cy_sems, cz_send, cz_recv, cr_send, cr_recv, cf_sems, cs_sems,
):
    x, y, z, core = place(nz)
    other = 1 - core
    chips = nx * ny
    here = x * ny + y
    half = D // 2
    head_rows = D // nx
    g_rows = half // ny
    c_rows = half // chips
    g_tile = g_rows // TILES
    c_tile = 2 * c_rows // TILES
    sibling = {"corpus": (y * nz + z) * 2 + other, "query": x}

    def chip(g):
        return {"corpus": (lax.rem(g, ny) * nz + z) * 2 + core, "query": g // ny}

    def far(o):
        return {"corpus": (y * nz + o) * 2 + core, "query": x}

    def copy(src, dst, send, recv, device):
        return pltpu.make_async_remote_copy(
            src_ref=src, dst_ref=dst, send_sem=send, recv_sem=recv, device_id=device, device_id_type=MESH
        )

    def loop(start, count, act):
        def body(d, carry):
            act(d)
            return carry

        lax.fori_loop(start, count, body, 0)

    def at_chip(d):
        return lax.rem(here + d, chips)

    def from_chip(d):
        return lax.rem(here + chips - d, chips)

    def at_y(d):
        return lax.rem(y + d, ny)

    barrier = pltpu.get_barrier_semaphore()
    pl.semaphore_signal(barrier, 1, device_id=sibling, device_id_type=MESH)
    loop(1, chips, lambda d: pl.semaphore_signal(barrier, 1, device_id=chip(at_chip(d)), device_id_type=MESH))
    loop(1, nz, lambda d: pl.semaphore_signal(barrier, 1, device_id=far(lax.rem(z + d, nz)), device_id_type=MESH))
    pl.semaphore_wait(barrier, chips + nz - 1)

    def g_core_copy(d):
        rows = pl.ds(pl.multiple_of(other * half + at_y(d) * g_rows, 8), g_rows)
        return copy(grad_ref.at[rows], g_core.at[d], gc_sems.at[0, d], gc_sems.at[1, d], sibling)

    def c_core_copy(d):
        rows = pl.ds(pl.multiple_of(other * half + at_chip(d) * c_rows, 8), c_rows)
        return copy(book_ref.at[rows], c_core.at[d], cc_sems.at[0, d], cc_sems.at[1, d], sibling)

    def q_copy(d):
        to = lax.rem(x + d, nx)
        rows = pl.ds(pl.multiple_of(to * head_rows, 16), head_rows)
        device = {"corpus": lax.axis_index("corpus"), "query": to}
        return copy(qint_ref.at[rows], q_all.at[x], q_sems.at[0, d], q_sems.at[1, d], device)

    def g_y_copy(d):
        device = {"corpus": (at_y(d) * nz + z) * 2 + core, "query": x}
        return copy(g_send.at[d], g_block.at[d], gy_sems.at[0, d], gy_sems.at[1, d], device)

    def c_chip_copy(d):
        return copy(c_send.at[d], c_block.at[d], cy_sems.at[0, d], cy_sems.at[1, d], chip(at_chip(d)))

    def g_part(t):
        return (pl.ds(t * g_tile, g_tile), slice(None))

    def c_part(t):
        return (pl.ds((t // 2) * c_tile, c_tile), pl.ds((t % 2) * LANES, LANES))

    def g_owner(t):
        return (t * nz) // TILES

    def c_owner(t):
        return ((2 * t + 1) * nz) // (2 * TILES)

    def slot(owner, t):
        return sum(1 for s in range(t) if owner(s) == owner(t))

    def z_copy(t, send, recv, owner, part, z_in, z_send, z_recv):
        return copy(
            send.at[part(t)], z_in.at[slot(owner, t), z], z_send.at[t], z_recv.at[slot(owner, t), z], far(owner(t))
        )

    def z_heard(t, o, owner, z_in, z_send, z_recv):
        tile = z_in.at[slot(owner, t), o]
        return copy(tile, tile, z_send.at[t], z_recv.at[slot(owner, t), o], far(o))

    g_final = g_fin.at[x, core, y]
    c_final = c_fin.at[core, here]

    def scatter_z(total, owner, part, z_in, z_send, z_recv):
        for t in range(TILES):
            mine = z == owner(t)

            @pl.when(mine)
            def _(t=t):
                z_in[slot(owner, t), z] = total[part(t)]

            @pl.when(jnp.logical_not(mine))
            def _(t=t):
                z_copy(t, total, None, owner, part, z_in, z_send, z_recv).start()

    def reduced_copy(t, d, owner, part, red, final, send, recv):
        return copy(
            red.at[slot(owner, t)], final.at[part(t)], send.at[slot(owner, t), d], recv.at[t],
            far(lax.rem(z + d, nz)),
        )

    def reduce_z(owner, part, z_in, z_send, z_recv, red, final, send, recv, dtype):
        for t in range(TILES):

            @pl.when(z == owner(t))
            def _(t=t):
                loop(1, nz, lambda d: z_heard(t, lax.rem(z + d, nz), owner, z_in, z_send, z_recv).wait_recv())
                whole = jnp.sum(z_in[slot(owner, t)], axis=0).astype(dtype)
                red[slot(owner, t)] = whole
                loop(1, nz, lambda d: reduced_copy(t, d, owner, part, red, final, send, recv).start())
                final[part(t)] = whole

    def heard_z(owner, part, red, final, send, recv):
        for t in range(TILES):

            @pl.when(z != owner(t))
            def _(t=t):
                reduced_copy(t, 0, owner, part, red, final, send, recv).wait_recv()

    def sent_z(total, owner, part, z_in, z_send, z_recv, red, final, send, recv):
        for t in range(TILES):
            mine = z == owner(t)

            @pl.when(mine)
            def _(t=t):
                loop(1, nz, lambda d: reduced_copy(t, d, owner, part, red, final, send, recv).wait_send())

            @pl.when(jnp.logical_not(mine))
            def _(t=t):
                z_copy(t, total, None, owner, part, z_in, z_send, z_recv).wait_send()

    def g_out(d):
        return copy(g_final, g_final, gf_sems.at[0, d], gf_sems.at[1, d], chip(at_chip(d)))

    def g_in(d):
        there = from_chip(d)
        block = g_fin.at[there // ny, core, lax.rem(there, ny)]
        return copy(block, block, gf_sems.at[0, d], gf_sems.at[1, d], chip(there))

    def g_share(d):
        there = from_chip(d)
        block = g_fin.at[there // ny, core, lax.rem(there, ny)]
        return copy(block, block, gs_sems.at[0, d], gs_sems.at[1, d], sibling)

    def g_shared(d):
        there = from_chip(d)
        block = g_fin.at[there // ny, other, lax.rem(there, ny)]
        return copy(block, block, gs_sems.at[0, d], gs_sems.at[1, d], sibling)

    def c_out(d):
        return copy(c_final, c_final, cf_sems.at[0, d], cf_sems.at[1, d], chip(at_chip(d)))

    def c_in(d):
        block = c_fin.at[core, from_chip(d)]
        return copy(block, block, cf_sems.at[0, d], cf_sems.at[1, d], chip(from_chip(d)))

    def c_share(d):
        block = c_fin.at[core, from_chip(d)]
        return copy(block, block, cs_sems.at[0, d], cs_sems.at[1, d], sibling)

    def c_shared(d):
        block = c_fin.at[other, from_chip(d)]
        return copy(block, block, cs_sems.at[0, d], cs_sems.at[1, d], sibling)

    loop(1, ny, lambda d: g_core_copy(d).start())
    g_core_copy(0).start()
    loop(1, chips, lambda d: c_core_copy(d).start())
    c_core_copy(0).start()
    loop(1, nx, lambda d: q_copy(d).start())
    q_all[x] = qint_ref[pl.ds(pl.multiple_of(x * head_rows, 16), head_rows), :]

    def g_forward(d):
        g_core_copy(d).wait_recv()
        rows = pl.ds(pl.multiple_of(core * half + at_y(d) * g_rows, 8), g_rows)
        g_send[d] = grad_ref[rows, :] + g_core[d]

    def g_go(d):
        g_forward(d)
        g_y_copy(d).start()

    def c_forward(d):
        c_core_copy(d).wait_recv()
        rows = pl.ds(pl.multiple_of(core * half + at_chip(d) * c_rows, 8), c_rows)
        c_send[d] = book_ref[rows, :] + c_core[d]

    def c_go(d):
        c_forward(d)
        c_chip_copy(d).start()

    loop(1, ny, g_go)
    g_forward(0)
    loop(1, chips, c_go)
    c_forward(0)

    g_args = (g_owner, g_part, g_z, gz_send, gz_recv)
    c_args = (c_owner, c_part, c_z, cz_send, cz_recv)
    g_more = (g_red, g_final, gr_send, gr_recv)
    c_more = (c_red, c_final, cr_send, cr_recv)
    loop(1, ny, lambda d: g_y_copy(d).wait_recv())
    total = g_send[0]
    for d in range(1, ny):
        total = total + g_block[d]
    g_sum[...] = total
    scatter_z(g_sum, *g_args)
    loop(1, chips, lambda d: c_chip_copy(d).wait_recv())
    total = c_send[0]
    for d in range(1, chips):
        total = total + c_block[d]
    c_sum[...] = total
    scatter_z(c_sum, *c_args)
    reduce_z(*g_args, *g_more, jnp.bfloat16)
    reduce_z(*c_args, *c_more, jnp.float32)

    heard_z(g_owner, g_part, *g_more)
    loop(1, chips, lambda d: g_out(d).start())
    g_share(0).start()
    heard_z(c_owner, c_part, *c_more)
    loop(1, chips, lambda d: c_out(d).start())
    c_share(0).start()

    def g_pass(d):
        g_in(d).wait_recv()
        g_share(d).start()

    def c_pass(d):
        c_in(d).wait_recv()
        c_share(d).start()

    loop(1, chips, g_pass)
    loop(1, chips, c_pass)
    loop(0, chips, lambda d: g_shared(d).wait_recv())
    loop(1, nx, lambda d: q_copy(d).wait_recv())
    head = jnp.zeros((head_rows, D), jnp.float32)
    for o in range(nx):
        head = head + lax.dot_general(
            q_all[o], g_fin[o].reshape(D, Q_DEV), NT, preferred_element_type=jnp.float32
        )
    head_ref[...] = head
    loop(0, chips, lambda d: c_shared(d).wait_recv())
    out_ref[...] = c_fin[...].reshape(D, K)

    loop(0, ny, lambda d: g_core_copy(d).wait_send())
    loop(0, chips, lambda d: c_core_copy(d).wait_send())
    loop(1, nx, lambda d: q_copy(d).wait_send())
    loop(1, ny, lambda d: g_y_copy(d).wait_send())
    loop(1, chips, lambda d: c_chip_copy(d).wait_send())
    sent_z(g_sum, *g_args, *g_more)
    sent_z(c_sum, *c_args, *c_more)
    loop(1, chips, lambda d: g_out(d).wait_send())
    loop(0, chips, lambda d: g_share(d).wait_send())
    loop(1, chips, lambda d: c_out(d).wait_send())
    loop(0, chips, lambda d: c_share(d).wait_send())


def device_sums(nx, ny, nz, grad, book, qint):
    whole = pl.BlockSpec(memory_space=pltpu.VMEM)
    dma = pltpu.SemaphoreType.DMA
    f32, bf16 = jnp.float32, jnp.bfloat16
    chips = nx * ny
    per = -(-TILES // nz)
    g_rows, c_rows = D // 2 // ny, D // 2 // chips
    g_tile, c_tile = g_rows // TILES, 2 * c_rows // TILES
    return pl.pallas_call(
        functools.partial(sums_kernel, nx, ny, nz),
        out_shape=[
            jax.ShapeDtypeStruct((D // nx, D), f32),
            jax.ShapeDtypeStruct((D, K), f32),
        ],
        in_specs=[whole] * 3,
        out_specs=[whole] * 2,
        scratch_shapes=[
            pltpu.VMEM((nx, D // nx, Q_DEV), bf16),
            pltpu.VMEM((ny, g_rows, Q_DEV), f32),
            pltpu.VMEM((ny, g_rows, Q_DEV), f32),
            pltpu.VMEM((ny, g_rows, Q_DEV), f32),
            pltpu.VMEM((g_rows, Q_DEV), f32),
            pltpu.VMEM((per, nz, g_tile, LANES), f32),
            pltpu.VMEM((per, g_tile, LANES), bf16),
            pltpu.VMEM((nx, 2, ny, g_rows, Q_DEV), bf16),
            pltpu.VMEM((chips, c_rows, K), f32),
            pltpu.VMEM((chips, c_rows, K), f32),
            pltpu.VMEM((chips, c_rows, K), f32),
            pltpu.VMEM((c_rows, K), f32),
            pltpu.VMEM((per, nz, c_tile, LANES), f32),
            pltpu.VMEM((per, c_tile, LANES), f32),
            pltpu.VMEM((2, chips, c_rows, K), f32),
            dma((2, nx)),
            dma((2, ny)),
            dma((2, ny)),
            dma((TILES,)),
            dma((per, nz)),
            dma((per, nz)),
            dma((TILES,)),
            dma((2, chips)),
            dma((2, chips)),
            dma((2, chips)),
            dma((2, chips)),
            dma((TILES,)),
            dma((per, nz)),
            dma((per, nz)),
            dma((TILES,)),
            dma((2, chips)),
            dma((2, chips)),
        ],
        compiler_params=pltpu.CompilerParams(
            collective_id=1, has_side_effects=True, vmem_limit_bytes=VMEM_BYTES
        ),
    )(grad, book, qint)


def shards(sizes, queries_in, head_weight, codebook, codes, slab_sizes, positive_ids):
    nx, ny, nz = sizes
    cent = codebook.reshape(M, K, SUB).transpose(0, 2, 1).reshape(D, K).astype(jnp.float32)
    ids = positive_ids.reshape(1, Q_DEV)
    qt, qint, pt, st, codest, stats = local_scores(slab_sizes, queries_in, head_weight, cent, codes, ids)
    totals = query_totals(ny, nz, stats)
    grad, book = local_grads(ids, totals, qt, pt, st, codest)
    head_grad, book = device_sums(nx, ny, nz, grad, book, qint)
    flat_book = book.reshape(M, SUB, K).transpose(0, 2, 1).reshape(M, K * SUB)
    return (totals[1], head_grad, flat_book)


def solution(mesh):
    return jax.shard_map(
        functools.partial(shards, grid_of(mesh)),
        mesh=mesh,
        in_specs=(P("query", None), P(), P(), P("corpus", None), P("corpus"), P("query")),
        out_specs=(P("query"), P("query", None), P()),
        check_vma=False,
    )
```

time: 1120 us -> 99.5 us (0.09)
  blocking collectives: 993 us -> 0 us
  Pallas kernels: 0 us -> 86.9 us
  matrix products: 50.7 us -> 0 us
  waiting for transfers between devices: 30.1 us -> 0 us
  between operations: 16.8 us -> 1.36 us
    psum x2 -> x0, blocking collectives: 738 us -> none  [shards(): totals, pos_total = lax.psum((local_total, pos_score), 'corpus')]
    pmax x1 -> x0, blocking collectives: 255 us -> none  [shards(): row_peak = lax.pmax(local_peak, 'corpus')]
    pallas_call x0 -> x4, Pallas kernels: none -> 86.9 us  [the longest x1 50.1 us: device_sums(): pl.pallas_call(functools.partial(sums_kernel, nx, ny, nz), out_shape=[jax...]
    dot_general x41 -> x0, matrix products: 50.7 us -> none  [the longest x12 15.6 us: book_terms(): jnp.einsum('rgs,rgk->gsk', lower[:, first_sub:first_sub + GROUP], onehot,...]
    unnamed x3 -> x0, waiting for transfers between devices: 30.1 us -> none
  transfers between devices with their start and end apart: 2 -> 0, of which waited for: 1 -> 0; matrix products, arithmetic and copies ran while one was open for 1% -> 0% of each run, Pallas kernels for 0% -> 0%
where the time goes in v1:
time: 99.5 us; the launch traced here: 99.2 us
  Pallas kernels  86.9 us (87%)
  local copies, waits for them, and re-layouts  10.9 us (11%)
  between operations  1.36 us (1%)
    pallas_call x1, Pallas kernels, device_sums(): pl.pallas_call(functools.partial(sums_kernel, nx, ny, nz), out_shape=[jax...  50.1 us
    pallas_call x1, Pallas kernels, query_totals(): pl.pallas_call(functools.partial(totals_kernel, ny, nz), out_shape=jax.Sh...  27.3 us
    pallas_call x1, Pallas kernels, local_grads(): pl.pallas_call(grad_kernel, out_shape=[jax.ShapeDtypeStruct((D, Q_DEV), j...  6.94 us
    unnamed x17, local copies, waits for them, and re-layouts  5.93 us
    convert_element_type x2, local copies, waits for them, and re-layouts, shards(): codebook.reshape(M, K, SUB).transpose(0, 2, 1).reshape(D, K)  3.96 us
    pallas_call x1, Pallas kernels, local_scores(): pl.pallas_call(score_kernel, out_shape=[jax.ShapeDtypeStruct((D, Q_DEV),...  2.56 us

profile of v1, /device:TPU:1, one launch (start us, length us, event | category | flops | bytes accessed | tf_op | source)
XLA Modules:
  0.0 99.2 jit_solution(13139451262564185787)
XLA Ops:
  1.3 1.0 %copy.14.codes_ref = s32[384,96]{1,0:T(8,128)S(1)} copy(s32[384,96]{0,1:T(8,128)} %param.9) | data formatting | bytes 294912 | tf_op args[3]
  2.3 2.2 %copy.12 = f32[96,2048]{0,1:T(8,128)} copy(bf16[96,2048]{1,0:T(8,128)(2,1)} %param.8) | data formatting | bytes 1179648 | tf_op jit(solution)/shard_map/convert_element_type | solution.py:568
  4.5 0.0 copy-start
  4.5 0.0 copy-start.1
  4.5 0.0 copy-start.6
  4.5 1.8 %copy.13 = f32[96,8,256]{2,1,0:T(8,128)S(1)} copy(f32[96,8,256]{0,1,2:T(8,128)} %bitcast.16) | data formatting | bytes 1572864 | tf_op jit(solution)/shard_map/convert_element_type | solution.py:568
  6.3 0.0 copy-done
  6.3 0.0 copy-done.1
  6.3 0.0 copy-done.6
  6.3 2.6 %shard_map.85 = (bf16[768,128]{1,0:T(8,128)(2,1)S(1)}, bf16[768,128]{1,0:T(8,128)(2,1)S(1)}, bf16[768,384]{1,0:T(8,128)(2,1)S(1)}, f32[384,128]{1,0:T(8,128)S(1)...) custom-call(s32[1]{0:T(128)S(6)} %copy.18.length_ref, bf16[128,768]{1,0:T(8,128)(2,1)S(1)} %copy-done.1, ...), custom_call_target="tpu_custom_call" | custom-call | tf_op jit(solution)/shard_map/pallas_call | solution.py:85
  8.9 0.0 copy-start.2
  8.9 0.7 copy-done.2
  9.6 0.0 copy-start.5
  9.6 0.6 copy-done.5
  10.2 27.3 %shard_map.86.totals_ref = f32[8,128]{1,0:T(8,128)} custom-call(f32[8,128]{1,0:T(8,128)} %copy-done.5), custom_call_target="tpu_custom_call" | custom-call | tf_op jit(solution)/shard_map/pallas_call | solution.py:175
  37.5 0.0 copy-start.3
  37.5 0.9 copy-done.3
  38.4 0.0 copy-start.4
  38.4 0.7 copy-done.4
  39.1 6.9 %shard_map.87 = (f32[768,128]{1,0:T(8,128)S(1)}, f32[768,256]{1,0:T(8,128)S(1)}) custom-call(s32[1,128]{1,0:T(1,128)S(1)} %bitcast.14, f32[8,128]{1,0:T(8,128)S(1)} %copy-done.4, bf16[768,128]{1,0:T(8,128)(2,1)S(1)} %get-tuple-element.14.qt_ref, bf16[768,384]{1,0:T(8,128)(2,1)S(1)} %get-tuple-element.15.pt_ref, f32[384,128]{1,0:T(8,128)S(1)} %get-tuple-element.16.st_ref, ...), custom_call_target="tpu_custom_call" | custom-call | tf_op jit(solution)/shard_map/pallas_call | solution.py:226
  46.0 0.5 slice_bitcast_fusion
  46.6 50.1 %shard_map.88 = (f32[192,768]{1,0:T(8,128)S(1)}, f32[768,256]{1,0:T(8,128)S(1)}) custom-call(f32[768,128]{1,0:T(8,128)S(1)} %get-tuple-element.18.grad_ref, f32[768,256]{1,0:T(8,128)S(1)} %get-tuple-element.19.book_ref, bf16[768,128]{1,0:T(8,128)(2,1)S(1)} %get-tuple-element.20.qint_ref), custom_call_target="tpu_custom_call" | custom-call | tf_op jit(solution)/shard_map/pallas_call | solution.py:518
  96.7 0.5 copy.15
  97.2 1.2 %copy.16 = f32[96,2048]{1,0:T(8,128)} copy(f32[96,2048]{0,1:T(8,128)S(1)} %bitcast.15) | data formatting | bytes 1572864
  98.4 0.8 copy.19
Async XLA Ops:
  4.5 1.8 %copy-start = (bf16[768,768]{1,0:T(8,128)(2,1)S(1)}, bf16[768,768]{1,0:T(8,128)(2,1)}, u32[]{:S(2)}) copy-start(bf16[768,768]{1,0:T(8,128)(2,1)} %weight_ref.1) | copy-start | bytes 3538948
  4.5 1.8 %copy-start.1 = (bf16[128,768]{1,0:T(8,128)(2,1)S(1)}, bf16[128,768]{1,0:T(8,128)(2,1)}, u32[]{:S(2)}) copy-start(bf16[128,768]{1,0:T(8,128)(2,1)} %qin_ref.1) | copy-start | bytes 589828
  4.5 1.8 %copy-start.6 = (s32[128]{0:T(128)S(1)}, s32[128]{0:T(128)}, u32[]{:S(2)}) copy-start(s32[128]{0:T(128)} %param.11) | copy-start | bytes 1540
  8.9 0.7 copy-start.2
  9.6 0.6 copy-start.5
  37.5 0.9 copy-start.3
  38.4 0.7 copy-start.4

commit v2 on v0

v2 whole, which is shorter than its diff:
```python
import functools

import jax
import jax.numpy as jnp
from jax import lax
from jax.experimental import pallas as pl
from jax.experimental.pallas import tpu as pltpu
from jax.sharding import PartitionSpec as P

D = 768
M = 96
K = 256
SUB = 8
SLOT_DEV = 384
Q_DEV = 128
LANES = 128
NX = 4
NY = 4
CHIPS = NX * NY
HALF = D // 2
G_ROWS = HALF // NY
C_ROWS = HALF // CHIPS
C_SUBS = C_ROWS // SUB
HEAD_ROWS = D // NX
TILES = 6
G_TILE = G_ROWS // TILES
LAG = 3
NEAR = 2 * NY
MESH = pl.DeviceIdType.MESH
NT = (((1,), (1,)), ((), ()))
VMEM_BYTES = 64 * 1024 * 1024 - 65536


def loop(start, count, act):
    def body(step, carry):
        act(step)
        return carry

    lax.fori_loop(start, count, body, 0)


def spread(a):
    return 2 - a + 3 * (a // 2) - 2 * (a // 3)


def step_kernel(
    nz,
    length_ref, ids_hbm, qin_hbm, weight_hbm, codebook_hbm, codes_hbm,
    loss_ref, head_ref, out_ref,
    ids, qin, weight, codebook, codes, table, pt, qt, qint, pgt, stats, near, far, mid, book, grad,
    q_all, g_core, g_send, g_block, g_sum, g_z, g_red, g_fin,
    c_core, c_send, c_block, c_sum, c_z, c_red, c_fin,
    in_sems, near_sems, far_sems,
    q_sems, gc_sems, gy_sems, gz_send, gz_recv, gr_send, gr_recv, gf_sems, gs_sems,
    cc_sems, cy_sems, cz_send, cz_recv, cr_send, cr_recv, cf_sems, cs_sems,
):
    me = lax.axis_index("corpus")
    x, y, z, core = lax.axis_index("query"), me // (2 * nz), lax.rem(me // 2, nz), lax.rem(me, 2)
    other = 1 - core
    group = y * 2 + core

    def device(to_x, to_y, to_z, to_core):
        return {"corpus": (to_y * nz + to_z) * 2 + to_core, "query": to_x}

    sibling = device(x, y, z, other)

    def around(o):
        return device(x, o // 2, z, lax.rem(o, 2))

    def along(o):
        return device(x, y, o, core)

    def hop(e):
        return nz // 2 + ((e + 1) // 2) * (1 - 2 * lax.rem(e, 2))

    def chip_at(s, sign):
        to_x = lax.rem(x + 4 + sign * spread(s // 4), NX)
        to_y = lax.rem(y + 4 + sign * spread(lax.rem(s, 4)), NY)
        return to_x, to_y

    def place_at(s, sign):
        to_x, to_y = chip_at(s, sign)
        return to_x * NY + to_y

    def chip(s, sign=1):
        to_x, to_y = chip_at(s, sign)
        return device(to_x, to_y, z, core)

    def y_at(d):
        return lax.rem(y + d, NY)

    def copy(src, dst, send, recv, to):
        return pltpu.make_async_remote_copy(
            src_ref=src, dst_ref=dst, send_sem=send, recv_sem=recv, device_id=to, device_id_type=MESH
        )

    loads = [
        pltpu.make_async_copy(src, dst, in_sems.at[i])
        for i, (src, dst) in enumerate(
            [(codebook_hbm, codebook), (codes_hbm, codes), (qin_hbm, qin), (weight_hbm, weight), (ids_hbm, ids)]
        )
    ]
    for load in loads:
        load.start()
    barrier = pltpu.get_barrier_semaphore()

    def greet(to):
        pl.semaphore_signal(barrier, 1, device_id=to, device_id_type=MESH)

    loop(0, nz - 1, lambda e: greet(along(lax.rem(z + hop(e), nz))))
    loop(1, NEAR, lambda d: greet(around(lax.rem(group + d, NEAR))))
    loop(0, 12, lambda s: greet(chip(s)))

    loads[0].wait()
    wide = K * SUB // 2
    down = lax.broadcasted_iota(jnp.int32, (wide, wide), 0)
    across = lax.broadcasted_iota(jnp.int32, (wide, wide), 1)
    pick = down == (across % LANES) * SUB + across // LANES
    pick = jnp.where(pick, jnp.float32(1), jnp.float32(0)).astype(jnp.bfloat16)
    for part in range(2):
        words = jnp.dot(
            codebook[:, part * wide : (part + 1) * wide], pick, preferred_element_type=jnp.float32
        )
        for j in range(SUB):
            table[pl.ds(part * D + j, M, stride=SUB), :] = words[:, j * LANES : (j + 1) * LANES]
    loads[1].wait()

    def rebuild(pair, carry):
        halves = []
        for part in range(2):
            m = pair * 2 + part
            lower = table[pl.ds(pl.multiple_of(m * SUB, SUB), SUB), :]
            upper = table[pl.ds(pl.multiple_of(D + m * SUB, SUB), SUB), :]
            row = codes[pl.ds(m, 1), :]
            parts = []
            for tile in range(SLOT_DEV // LANES):
                index = jnp.broadcast_to(row[:, tile * LANES : (tile + 1) * LANES], (SUB, LANES))
                low = index & (LANES - 1)
                first = jnp.take_along_axis(lower, low, axis=1, mode="promise_in_bounds")
                second = jnp.take_along_axis(upper, low, axis=1, mode="promise_in_bounds")
                parts.append(jnp.where(index >= LANES, second, first))
            halves.append(jnp.concatenate(parts, axis=1))
        rows = jnp.concatenate(halves, axis=0).astype(jnp.bfloat16)
        pt[pl.ds(pl.multiple_of(pair * 2 * SUB, 2 * SUB), 2 * SUB), :] = rows
        return carry

    lax.fori_loop(0, M // 2, rebuild, 0, unroll=4)

    loads[2].wait()
    loads[3].wait()
    loads[4].wait()
    query = jnp.dot(qin[...], weight[...], preferred_element_type=jnp.float32).astype(jnp.bfloat16)
    scores = jnp.dot(query, pt[...], preferred_element_type=jnp.float32).T
    slot = lax.broadcasted_iota(jnp.int32, (SLOT_DEV, Q_DEV), 0)
    scores = jnp.where(slot < length_ref[0], scores, -jnp.inf)
    owned = slot == ids[...] - me * SLOT_DEV
    peak = jnp.max(scores, axis=0, keepdims=True)
    total = jnp.sum(jnp.exp(scores - peak), axis=0, keepdims=True)
    positive = jnp.sum(jnp.where(owned, scores, 0.0), axis=0, keepdims=True)
    pad = jnp.zeros((5, Q_DEV), jnp.float32)
    stats[...] = jnp.concatenate([peak, total, positive, pad], axis=0)
    pl.semaphore_wait(barrier, NEAR - 1 + nz - 1 + 12)

    def merge(slots):
        peaks, totals, positives = slots[:, 0, :], slots[:, 1, :], slots[:, 2, :]
        peak = jnp.max(peaks, axis=0, keepdims=True)
        total = jnp.sum(totals * jnp.exp(peaks - peak), axis=0, keepdims=True)
        return peak, total, jnp.sum(positives, axis=0, keepdims=True)

    def near_copy(d):
        to = around(lax.rem(group + d, NEAR))
        return copy(stats, near.at[group], near_sems.at[0, d], near_sems.at[1, d], to)

    def far_copy(e):
        to = along(lax.rem(z + hop(e), nz))
        return copy(mid, far.at[z], far_sems.at[0, e], far_sems.at[1, e], to)

    def q_copy(d):
        to = lax.rem(x + d, NX)
        rows = pl.ds(pl.multiple_of(to * HEAD_ROWS, 16), HEAD_ROWS)
        return copy(qint.at[rows], q_all.at[x], q_sems.at[0, d], q_sems.at[1, d], device(to, y, z, core))

    loop(1, NEAR, lambda d: near_copy(d).start())
    near[group] = stats[...]
    qt[...] = query.astype(jnp.float32).T.astype(jnp.bfloat16)
    qint[...] = qin[...].astype(jnp.float32).T.astype(jnp.bfloat16)
    loop(1, NEAR, lambda d: near_copy(d).wait_recv())
    mid[...] = jnp.concatenate([*merge(near[...]), pad], axis=0)
    loop(0, nz - 1, lambda e: far_copy(e).start())
    far[z] = mid[...]
    loop(1, NX, lambda d: q_copy(d).start())
    q_all[x] = qint[pl.ds(pl.multiple_of(x * HEAD_ROWS, 16), HEAD_ROWS), :]
    loop(0, nz - 1, lambda e: far_copy(e).wait_recv())
    peak, total, positive = merge(far[...])
    log_total = peak + jnp.log(total)
    loss_ref[...] = log_total - positive

    probs = jnp.exp(scores - log_total).astype(jnp.bfloat16)
    both = jnp.concatenate([probs, jnp.where(owned, -1.0, 0.0).astype(jnp.bfloat16)], axis=1)
    sides = jnp.dot(pt[...], both, preferred_element_type=jnp.float32)
    grad[...] = sides[:, :Q_DEV] + sides[:, Q_DEV:]

    def g_core_copy(d):
        rows = pl.ds(pl.multiple_of(other * HALF + y_at(d) * G_ROWS, 8), G_ROWS)
        return copy(grad.at[rows], g_core.at[d], gc_sems.at[0, d], gc_sems.at[1, d], sibling)

    loop(0, NY, lambda d: g_core_copy(lax.rem(d + 1, NY)).start())
    twice = jnp.concatenate([qt[...], qt[...]], axis=1)
    pgt[...] = lax.dot_general(twice, both, NT, preferred_element_type=jnp.float32)
    word = lax.broadcasted_iota(jnp.int32, (K, SLOT_DEV), 0).astype(jnp.float32)
    word = word.astype(jnp.bfloat16)

    def scatter(m):
        rows = pl.ds(pl.multiple_of(m * SUB, SUB), SUB)
        part = pgt[rows, :]
        upper = part.astype(jnp.bfloat16)
        lower = (part - upper.astype(jnp.float32)).astype(jnp.bfloat16)
        code = codes[pl.ds(m, 1), :].astype(jnp.float32).astype(jnp.bfloat16)
        onehot = jnp.where(word == code, jnp.bfloat16(1), jnp.bfloat16(0))
        halves = lax.dot_general(
            jnp.concatenate([upper, lower], axis=0), onehot, NT, preferred_element_type=jnp.float32
        )
        book[rows, :] = halves[:SUB] + halves[SUB:]

    def c_rows(s, side):
        return pl.ds(pl.multiple_of(side * HALF + place_at(s, 1) * C_ROWS, 8), C_ROWS)

    def c_core_copy(s):
        return copy(
            book.at[c_rows(s, other)], c_core.at[s], cc_sems.at[0, s], cc_sems.at[1, s], sibling
        )

    def c_chip_copy(s):
        return copy(c_send.at[s], c_block.at[s], cy_sems.at[0, s], cy_sems.at[1, s], chip(s))

    def c_compute(s):
        for side in (other, core):
            first = side * (M // 2) + place_at(s, 1) * C_SUBS
            for i in range(C_SUBS):
                scatter(first + i)
            if side is other:
                c_core_copy(s).start()

    def c_finish(s):
        c_core_copy(s).wait_recv()
        c_send[s] = book[c_rows(s, core), :] + c_core[s]

    def c_go(s):
        c_finish(s)
        c_chip_copy(s).start()

    def c_both(s):
        c_compute(s)
        c_go(s - LAG)

    def g_y_copy(d):
        return copy(g_send.at[d], g_block.at[d], gy_sems.at[0, d], gy_sems.at[1, d], device(x, y_at(d), z, core))

    def g_finish(d):
        g_core_copy(d).wait_recv()
        rows = pl.ds(pl.multiple_of(core * HALF + y_at(d) * G_ROWS, 8), G_ROWS)
        g_send[d] = grad[rows, :] + g_core[d]

    def g_go(d):
        g_finish(d)
        g_y_copy(d).start()

    def g_part(t):
        return (pl.ds(t * G_TILE, G_TILE), slice(None))

    def c_part(t):
        return (pl.ds((t // 2) * SUB, SUB), pl.ds((t % 2) * LANES, LANES))

    def c_out_part(t):
        return (pl.ds(t * SUB, SUB), slice(None))

    def g_owner(t):
        return (t * nz) // TILES

    def c_owner(t):
        return ((2 * t + 1) * nz) // (2 * TILES)

    def place(owner, t):
        return sum(1 for s in range(t) if owner(s) == owner(t))

    def z_copy(t, total, owner, part, z_in, z_send, z_recv):
        p = place(owner, t)
        return copy(total.at[part(t)], z_in.at[p, z], z_send.at[t], z_recv.at[p, z], along(owner(t)))

    def z_heard(t, o, owner, z_in, z_send, z_recv):
        p = place(owner, t)
        return copy(z_in.at[p, o], z_in.at[p, o], z_send.at[t], z_recv.at[p, o], along(o))

    def scatter_z(total, owner, part, z_in, z_send, z_recv):
        for t in range(TILES):
            mine = z == owner(t)

            @pl.when(mine)
            def _(t=t):
                z_in[place(owner, t), z] = total[part(t)]

            @pl.when(jnp.logical_not(mine))
            def _(t=t):
                z_copy(t, total, owner, part, z_in, z_send, z_recv).start()

    def back_copy(t, e, owner, part, red, final, send, recv):
        p = place(owner, t)
        to = along(lax.rem(z + hop(e), nz))
        return copy(red.at[p], final.at[part(t)], send.at[p, e], recv.at[t], to)

    def reduce_z(shape, owner, z_in, z_send, z_recv, part, red, final, send, recv):
        for t in range(TILES):

            @pl.when(z == owner(t))
            def _(t=t):
                loop(
                    0, nz - 1,
                    lambda e: z_heard(t, lax.rem(z + hop(e), nz), owner, z_in, z_send, z_recv).wait_recv(),
                )
                whole = shape(jnp.sum(z_in[place(owner, t)], axis=0))
                red[place(owner, t)] = whole
                loop(0, nz - 1, lambda e: back_copy(t, e, owner, part, red, final, send, recv).start())
                final[part(t)] = whole

    def heard_z(owner, part, red, final, send, recv):
        for t in range(TILES):

            @pl.when(z != owner(t))
            def _(t=t):
                back_copy(t, 0, owner, part, red, final, send, recv).wait_recv()

    def sent_z(total, owner, part, z_in, z_send, z_recv, out_part, red, final, send, recv):
        for t in range(TILES):
            mine = z == owner(t)

            @pl.when(mine)
            def _(t=t):
                loop(0, nz - 1, lambda e: back_copy(t, e, owner, out_part, red, final, send, recv).wait_send())

            @pl.when(jnp.logical_not(mine))
            def _(t=t):
                z_copy(t, total, owner, part, z_in, z_send, z_recv).wait_send()

    def interleave(tile):
        down = lax.broadcasted_iota(jnp.int32, (SUB, LANES), 0)
        across = lax.broadcasted_iota(jnp.int32, (SUB, LANES), 1)
        index = down * (LANES // SUB) + across // SUB
        mixed = jnp.zeros((SUB, LANES), jnp.float32)
        for j in range(SUB):
            row = jnp.broadcast_to(tile[j : j + 1, :], (SUB, LANES))
            row = jnp.take_along_axis(row, index, axis=1, mode="promise_in_bounds")
            mixed = jnp.where(across % SUB == j, row, mixed)
        return mixed

    loop(0, LAG, c_compute)
    loop(1, NY, g_go)
    g_finish(0)
    loop(LAG, 10, c_both)
    loop(1, NY, lambda d: g_y_copy(d).wait_recv())
    g_total = g_send[0]
    for d in range(1, NY):
        g_total = g_total + g_block[d]
    g_sum[...] = g_total
    g_final = g_fin.at[x, core, y]
    g_way = (g_owner, g_part, g_z, gz_send, gz_recv)
    g_back = (g_red, g_final, gr_send, gr_recv)
    scatter_z(g_sum, *g_way)
    loop(10, CHIPS, c_both)
    loop(CHIPS - LAG, CHIPS - 1, c_go)
    c_finish(CHIPS - 1)

    loop(0, CHIPS - 1, lambda s: c_chip_copy(s).wait_recv())
    c_total = c_send[CHIPS - 1]
    for s in range(CHIPS - 1):
        c_total = c_total + c_block[s]
    c_sum[...] = c_total

    def c_final_at(side, place):
        return c_fin.at[pl.ds(pl.multiple_of((side * CHIPS + place) * 2 * C_ROWS, 8), 2 * C_ROWS)]

    c_final = c_final_at(core, x * NY + y)
    c_way = (c_owner, c_part, c_z, cz_send, cz_recv)
    c_back = (c_red, c_final, cr_send, cr_recv)
    scatter_z(c_sum, *c_way)
    reduce_z(lambda a: a.astype(jnp.bfloat16), g_owner, *g_way[2:], g_part, *g_back)
    reduce_z(interleave, c_owner, *c_way[2:], c_out_part, *c_back)

    def g_at(side, s):
        from_x, from_y = chip_at(s, -1)
        return g_fin.at[from_x, side, from_y]

    def g_out(s):
        return copy(g_final, g_final, gf_sems.at[0, s], gf_sems.at[1, s], chip(s))

    def g_in(s):
        return copy(g_at(core, s), g_at(core, s), gf_sems.at[0, s], gf_sems.at[1, s], chip(s))

    def g_share(s):
        return copy(g_at(core, s), g_at(core, s), gs_sems.at[0, s], gs_sems.at[1, s], sibling)

    def g_shared(s):
        return copy(g_at(other, s), g_at(other, s), gs_sems.at[0, s], gs_sems.at[1, s], sibling)

    def c_out(s):
        return copy(c_final, c_final, cf_sems.at[0, s], cf_sems.at[1, s], chip(s))

    def c_at(side, s):
        return c_final_at(side, place_at(s, -1))

    def c_in(s):
        return copy(c_at(core, s), c_at(core, s), cf_sems.at[0, s], cf_sems.at[1, s], chip(s))

    def c_share(s):
        return copy(c_at(core, s), c_at(core, s), cs_sems.at[0, s], cs_sems.at[1, s], sibling)

    def c_shared(s):
        return copy(c_at(other, s), c_at(other, s), cs_sems.at[0, s], cs_sems.at[1, s], sibling)

    heard_z(g_owner, g_part, *g_back)
    loop(0, CHIPS - 1, lambda s: g_out(s).start())
    g_share(CHIPS - 1).start()
    heard_z(c_owner, c_out_part, *c_back)
    loop(0, CHIPS - 1, lambda s: c_out(s).start())
    c_share(CHIPS - 1).start()

    def g_pass(s):
        g_in(s).wait_recv()
        g_share(s).start()

    def c_pass(s):
        c_in(s).wait_recv()
        c_share(s).start()

    loop(0, CHIPS - 1, g_pass)
    loop(0, CHIPS, lambda s: g_shared(s).wait_recv())
    loop(1, NX, lambda d: q_copy(d).wait_recv())
    head = jnp.zeros((HEAD_ROWS, D), jnp.float32)
    for o in range(NX):
        head = head + lax.dot_general(
            q_all[o], g_fin[o].reshape(D, Q_DEV), NT, preferred_element_type=jnp.float32
        )
    head_ref[...] = head
    loop(0, CHIPS - 1, c_pass)
    loop(0, CHIPS, lambda s: c_shared(s).wait_recv())
    for u in range(2 * SUB):
        out_ref[:, u * LANES : (u + 1) * LANES] = c_fin[pl.ds(u, M, stride=2 * SUB), :]

    loop(1, NEAR, lambda d: near_copy(d).wait_send())
    loop(0, nz - 1, lambda e: far_copy(e).wait_send())
    loop(1, NX, lambda d: q_copy(d).wait_send())
    loop(0, NY, lambda d: g_core_copy(d).wait_send())
    loop(0, CHIPS, lambda s: c_core_copy(s).wait_send())
    loop(1, NY, lambda d: g_y_copy(d).wait_send())
    loop(0, CHIPS - 1, lambda s: c_chip_copy(s).wait_send())
    sent_z(g_sum, *g_way, g_part, *g_back)
    sent_z(c_sum, *c_way, c_out_part, *c_back)
    loop(0, CHIPS - 1, lambda s: g_out(s).wait_send())
    loop(0, CHIPS, lambda s: g_share(s).wait_send())
    loop(0, CHIPS - 1, lambda s: c_out(s).wait_send())
    loop(0, CHIPS, lambda s: c_share(s).wait_send())


def step(nz, queries_in, head_weight, codebook, codes, slab_sizes, positive_ids):
    whole = pl.BlockSpec(memory_space=pltpu.VMEM)
    left = pl.BlockSpec(memory_space=pltpu.HBM)
    dma = pltpu.SemaphoreType.DMA
    f32, bf16 = jnp.float32, jnp.bfloat16
    per = -(-TILES // nz)
    loss, head_grad, book = pl.pallas_call(
        functools.partial(step_kernel, nz),
        out_shape=[
            jax.ShapeDtypeStruct((1, Q_DEV), f32),
            jax.ShapeDtypeStruct((HEAD_ROWS, D), f32),
            jax.ShapeDtypeStruct((M, K * SUB), f32),
        ],
        in_specs=[pl.BlockSpec(memory_space=pltpu.SMEM)] + [left] * 5,
        out_specs=[whole] * 3,
        scratch_shapes=[
            pltpu.VMEM((1, Q_DEV), jnp.int32),
            pltpu.VMEM((Q_DEV, D), bf16),
            pltpu.VMEM((D, D), bf16),
            pltpu.VMEM((M, K * SUB), bf16),
            pltpu.VMEM((M, SLOT_DEV), jnp.int32),
            pltpu.VMEM((2 * D, LANES), f32),
            pltpu.VMEM((D, SLOT_DEV), bf16),
            pltpu.VMEM((D, Q_DEV), bf16),
            pltpu.VMEM((D, Q_DEV), bf16),
            pltpu.VMEM((D, SLOT_DEV), f32),
            pltpu.VMEM((8, Q_DEV), f32),
            pltpu.VMEM((NEAR, 8, Q_DEV), f32),
            pltpu.VMEM((nz, 8, Q_DEV), f32),
            pltpu.VMEM((8, Q_DEV), f32),
            pltpu.VMEM((D, K), f32),
            pltpu.VMEM((D, Q_DEV), f32),
            pltpu.VMEM((NX, HEAD_ROWS, Q_DEV), bf16),
            pltpu.VMEM((NY, G_ROWS, Q_DEV), f32),
            pltpu.VMEM((NY, G_ROWS, Q_DEV), f32),
            pltpu.VMEM((NY, G_ROWS, Q_DEV), f32),
            pltpu.VMEM((G_ROWS, Q_DEV), f32),
            pltpu.VMEM((per, nz, G_TILE, LANES), f32),
            pltpu.VMEM((per, G_TILE, LANES), bf16),
            pltpu.VMEM((NX, 2, NY, G_ROWS, Q_DEV), bf16),
            pltpu.VMEM((CHIPS, C_ROWS, K), f32),
            pltpu.VMEM((CHIPS, C_ROWS, K), f32),
            pltpu.VMEM((CHIPS, C_ROWS, K), f32),
            pltpu.VMEM((C_ROWS, K), f32),
            pltpu.VMEM((per, nz, SUB, LANES), f32),
            pltpu.VMEM((per, SUB, LANES), f32),
            pltpu.VMEM((2 * D, LANES), f32),
            dma((5,)),
            dma((2, NEAR)),
            dma((2, nz)),
            dma((2, NX)),
            dma((2, NY)),
            dma((2, NY)),
            dma((TILES,)),
            dma((per, nz)),
            dma((per, nz)),
            dma((TILES,)),
            dma((2, CHIPS)),
            dma((2, CHIPS)),
            dma((2, CHIPS)),
            dma((2, CHIPS)),
            dma((TILES,)),
            dma((per, nz)),
            dma((per, nz)),
            dma((TILES,)),
            dma((2, CHIPS)),
            dma((2, CHIPS)),
        ],
        compiler_params=pltpu.CompilerParams(
            collective_id=0, has_side_effects=True, vmem_limit_bytes=VMEM_BYTES
        ),
    )(slab_sizes, positive_ids.reshape(1, Q_DEV), queries_in, head_weight, codebook, codes.T)
    return loss.reshape(Q_DEV), head_grad, book


def solution(mesh):
    nz = mesh.shape["corpus"] // (2 * NY)
    return jax.shard_map(
        functools.partial(step, nz),
        mesh=mesh,
        in_specs=(P("query", None), P(), P(), P("corpus", None), P("corpus"), P("query")),
        out_specs=(P("query"), P("query", None), P()),
        check_vma=False,
    )
```

time: 1120 us -> 75.8 us (0.07)
  blocking collectives: 993 us -> 0 us
  Pallas kernels: 0 us -> 70.3 us
  matrix products: 50.7 us -> 0 us
  waiting for transfers between devices: 30.1 us -> 0 us
  local copies, waits for them, and re-layouts: 22 us -> 3.96 us
  between operations: 16.8 us -> 1.3 us
    psum x2 -> x0, blocking collectives: 738 us -> none  [shards(): totals, pos_total = lax.psum((local_total, pos_score), 'corpus')]
    pmax x1 -> x0, blocking collectives: 255 us -> none  [shards(): row_peak = lax.pmax(local_peak, 'corpus')]
    pallas_call x0 -> x1, Pallas kernels: none -> 70.3 us  [step(): pl.pallas_call(functools.partial(step_kernel, nz), out_shape=[jax.ShapeDt...]
    dot_general x41 -> x0, matrix products: 50.7 us -> none  [the longest x12 15.6 us: book_terms(): jnp.einsum('rgs,rgk->gsk', lower[:, first_sub:first_sub + GROUP], onehot,...]
    unnamed x3 -> x0, waiting for transfers between devices: 30.1 us -> none
  transfers between devices with their start and end apart: 2 -> 0, of which waited for: 1 -> 0; matrix products, arithmetic and copies ran while one was open for 1% -> 0% of each run, Pallas kernels for 0% -> 0%
where the time goes in v2:
time: 75.8 us; the launch traced here: 75.6 us
  Pallas kernels  70.3 us (93%)
  local copies, waits for them, and re-layouts  3.96 us (5%)
  between operations  1.3 us (2%)
    pallas_call x1, Pallas kernels, step(): pl.pallas_call(functools.partial(step_kernel, nz), out_shape=[jax.ShapeDt...  70.3 us
    unnamed x5, local copies, waits for them, and re-layouts  3.96 us

profile of v2, /device:TPU:1, one launch (start us, length us, event | category | flops | bytes accessed | tf_op | source)
XLA Modules:
  0.0 75.6 jit_solution(3786163383364202884)
XLA Ops:
  1.3 70.3 %shard_map.85 = (f32[1,128]{1,0:T(1,128)}, f32[192,768]{1,0:T(8,128)}, f32[96,2048]{1,0:T(8,128)}) custom-call(s32[1]{0:T(128)S(6)} %copy.12.length_ref, s32[1,128]{1,0:T(1,128)} %bitcast.4, bf16[128,768]{1,0:T(8,128)(2,1)} %qin_hbm.1, bf16[768,768]{1,0:T(8,128)(2,1)} %weight_hbm.1, bf16[96,2048]{1,0:T(8,128)(2,1)} %codebook_hbm.1, s32[96,384]{1,0:T(8,128)} %bitcast.3), custom_call_target="tpu_custom_call" | custom-call | tf_op jit(solution)/shard_map/pallas_call | solution.py:469
  71.6 0.0 copy-start
  71.6 1.2 %copy.13 = f32[128]{0:T(128)} copy(f32[128]{0:T(128)} %bitcast.5) | data formatting | bytes 1024
  72.8 1.9 %copy.14 = f32[192,768]{1,0:T(8,128)} copy(f32[192,768]{1,0:T(8,128)} %get-tuple-element.13) | data formatting | bytes 1179648
  74.7 0.0 copy-done
  74.7 0.9 %copy.15 = f32[96,2048]{1,0:T(8,128)} copy(f32[96,2048]{1,0:T(8,128)S(1)} %copy-done) | data formatting | bytes 1572864
Async XLA Ops:
  71.6 3.1 %copy-start = (f32[96,2048]{1,0:T(8,128)S(1)}, f32[96,2048]{1,0:T(8,128)}, u32[]{:S(2)}) copy-start(f32[96,2048]{1,0:T(8,128)} %get-tuple-element.14) | copy-start | bytes 2359300

commit v3 on v2

v3 whole, which is shorter than its diff:
```python
import functools

import jax
import jax.numpy as jnp
from jax import lax
from jax.experimental import pallas as pl
from jax.experimental.pallas import tpu as pltpu
from jax.sharding import PartitionSpec as P

D = 768
M = 96
K = 256
SUB = 8
SLOT_DEV = 384
Q_DEV = 128
LANES = 128
NX = 4
NY = 4
CHIPS = NX * NY
HALF = D // 2
G_ROWS = HALF // NY
C_ROWS = HALF // CHIPS
C_SUBS = C_ROWS // SUB
HEAD_ROWS = D // NX
TILES = 6
G_TILE = G_ROWS // TILES
NEAR = 2 * NY
MESH = pl.DeviceIdType.MESH
NT = (((1,), (1,)), ((), ()))
VMEM_BYTES = 64 * 1024 * 1024 - 65536


def loop(start, count, act):
    def body(step, carry):
        act(step)
        return carry

    lax.fori_loop(start, count, body, 0)


def spread(a):
    return 2 - a + 3 * (a // 2) - 2 * (a // 3)


def step_kernel(
    nz,
    length_ref, ids_hbm, qin_hbm, weight_hbm, codebook_hbm, codes_hbm,
    loss_hbm, head_hbm, out_hbm,
    ids, qin, weight, codebook, codes, table, pt, qt, qint, pgt, stats, near, far, mid, book,
    pu, sides, mass, fixed, scaled, loss, head, out,
    q_all, grad, g_core, g_send, g_block, g_sum, g_z, g_red, g_fin,
    c_core, c_send, c_block, c_sum, c_pair, c_half, c_many, c_fin,
    in_sems, out_sems, near_sems, far_sems,
    q_sems, gc_sems, gy_sems, gz_send, gz_recv, gr_send, gr_recv, gf_sems, gs_sems,
    cc_sems, cy_sems, cp_sems, cz_sems, cb_sems, cf_sems, cs_sems,
):
    me = lax.axis_index("corpus")
    x, y, z, core = lax.axis_index("query"), me // (2 * nz), lax.rem(me // 2, nz), lax.rem(me, 2)
    other = 1 - core
    group = y * 2 + core

    def device(to_x, to_y, to_z, to_core):
        return {"corpus": (to_y * nz + to_z) * 2 + to_core, "query": to_x}

    sibling = device(x, y, z, other)

    def around(o):
        return device(x, o // 2, z, lax.rem(o, 2))

    def along(o):
        return device(x, y, o, core)

    def hop(e, ring=nz):
        return ring // 2 + ((e + 1) // 2) * (1 - 2 * lax.rem(e, 2))

    def chip_at(s, sign):
        to_x = lax.rem(x + 4 + sign * spread(s // 4), NX)
        to_y = lax.rem(y + 4 + sign * spread(lax.rem(s, 4)), NY)
        return to_x, to_y

    def place_at(s, sign):
        to_x, to_y = chip_at(s, sign)
        return to_x * NY + to_y

    def chip(s, sign=1):
        to_x, to_y = chip_at(s, sign)
        return device(to_x, to_y, z, core)

    def y_at(d):
        return lax.rem(y + d, NY)

    def copy(src, dst, send, recv, to):
        return pltpu.make_async_remote_copy(
            src_ref=src, dst_ref=dst, send_sem=send, recv_sem=recv, device_id=to, device_id_type=MESH
        )

    barrier = pltpu.get_barrier_semaphore()

    def greet(to):
        pl.semaphore_signal(barrier, 1, device_id=to, device_id_type=MESH)

    loop(0, nz - 1, lambda e: greet(along(lax.rem(z + hop(e), nz))))
    loads = [
        pltpu.make_async_copy(src, dst, in_sems.at[i])
        for i, (src, dst) in enumerate(
            [(codebook_hbm, codebook), (codes_hbm, codes), (qin_hbm, qin), (weight_hbm, weight), (ids_hbm, ids)]
        )
    ]
    for load in loads:
        load.start()
    loop(1, NEAR, lambda d: greet(around(lax.rem(group + d, NEAR))))
    loop(0, 12, lambda s: greet(chip(s)))

    wide = K * SUB // 2
    down = lax.broadcasted_iota(jnp.int32, (wide, wide), 0)
    across = lax.broadcasted_iota(jnp.int32, (wide, wide), 1)
    pick = down == (across % LANES) * SUB + across // LANES
    pick = jnp.where(pick, jnp.float32(1), jnp.float32(0)).astype(jnp.bfloat16)
    loads[0].wait()
    for part in range(2):
        words = jnp.dot(
            codebook[:, part * wide : (part + 1) * wide], pick, preferred_element_type=jnp.float32
        )
        for j in range(SUB):
            table[pl.ds(part * D + j, M, stride=SUB), :] = words[:, j * LANES : (j + 1) * LANES]
    loads[1].wait()

    def rebuild(pair, carry):
        halves = []
        for part in range(2):
            m = pair * 2 + part
            lower = table[pl.ds(pl.multiple_of(m * SUB, SUB), SUB), :]
            upper = table[pl.ds(pl.multiple_of(D + m * SUB, SUB), SUB), :]
            row = codes[pl.ds(m, 1), :]
            parts = []
            for tile in range(SLOT_DEV // LANES):
                index = jnp.broadcast_to(row[:, tile * LANES : (tile + 1) * LANES], (SUB, LANES))
                low = index & (LANES - 1)
                first = jnp.take_along_axis(lower, low, axis=1, mode="promise_in_bounds")
                second = jnp.take_along_axis(upper, low, axis=1, mode="promise_in_bounds")
                parts.append(jnp.where(index >= LANES, second, first))
            halves.append(jnp.concatenate(parts, axis=1))
        rows = jnp.concatenate(halves, axis=0).astype(jnp.bfloat16)
        pt[pl.ds(pl.multiple_of(pair * 2 * SUB, 2 * SUB), 2 * SUB), :] = rows
        return carry

    lax.fori_loop(0, M // 2, rebuild, 0, unroll=4)

    loads[2].wait()
    loads[3].wait()
    loads[4].wait()
    query = jnp.dot(qin[...], weight[...], preferred_element_type=jnp.float32).astype(jnp.bfloat16)
    scores = jnp.dot(query, pt[...], preferred_element_type=jnp.float32).T
    slot = lax.broadcasted_iota(jnp.int32, (SLOT_DEV, Q_DEV), 0)
    scores = jnp.where(slot < length_ref[0], scores, -jnp.inf)
    owned = slot == ids[...] - me * SLOT_DEV
    peak = jnp.max(scores, axis=0, keepdims=True)
    raised = jnp.exp(scores - peak)
    total = jnp.sum(raised, axis=0, keepdims=True)
    positive = jnp.sum(jnp.where(owned, scores, 0.0), axis=0, keepdims=True)
    pad = jnp.zeros((5, Q_DEV), jnp.float32)
    stats[...] = jnp.concatenate([peak, total, positive, pad], axis=0)
    pl.semaphore_wait(barrier, NEAR - 1 + nz - 1 + 12)

    def merge(slots):
        peaks, totals, positives = slots[:, 0, :], slots[:, 1, :], slots[:, 2, :]
        peak = jnp.max(peaks, axis=0, keepdims=True)
        total = jnp.sum(totals * jnp.exp(peaks - peak), axis=0, keepdims=True)
        return peak, total, jnp.sum(positives, axis=0, keepdims=True)

    def near_copy(d):
        to = around(lax.rem(group + d, NEAR))
        return copy(stats, near.at[group], near_sems.at[0, d], near_sems.at[1, d], to)

    def far_copy(e):
        to = along(lax.rem(z + hop(e), nz))
        return copy(mid, far.at[z], far_sems.at[0, e], far_sems.at[1, e], to)

    def q_copy(d):
        to = lax.rem(x + d, NX)
        rows = pl.ds(pl.multiple_of(to * HEAD_ROWS, 16), HEAD_ROWS)
        return copy(qint.at[rows], q_all.at[x], q_sems.at[0, d], q_sems.at[1, d], device(to, y, z, core))

    def onto(m):
        rows = pl.ds(pl.multiple_of(m * SUB, SUB), SUB)
        part = pgt[rows, :]
        upper = part.astype(jnp.bfloat16)
        lower = (part - upper.astype(jnp.float32)).astype(jnp.bfloat16)
        code = codes[pl.ds(m, 1), :].astype(jnp.float32).astype(jnp.bfloat16)
        onehot = jnp.where(word == code, jnp.bfloat16(1), jnp.bfloat16(0))
        left = jnp.concatenate([pu[...], upper, lower], axis=0)
        sums = lax.dot_general(left, onehot, NT, preferred_element_type=jnp.float32)
        mass[pl.ds(pl.multiple_of(m * Q_DEV, Q_DEV), Q_DEV), :] = sums[:Q_DEV].astype(jnp.bfloat16)
        fixed[rows, :] = sums[Q_DEV : Q_DEV + SUB] + sums[Q_DEV + SUB :]

    def onto_range(first, last):
        def body(m, carry):
            onto(m)
            return carry

        lax.fori_loop(first, last, body, 0, unroll=4)

    def g_core_copy():
        rows = pl.ds(other * (HALF // 16), HALF // 16)
        return copy(grad.at[rows], g_core, gc_sems.at[0], gc_sems.at[1], sibling)

    def g_y_copy(d):
        to = device(x, y_at(d), z, core)
        return copy(g_send.at[d], g_block.at[d], gy_sems.at[0, d], gy_sems.at[1, d], to)

    def g_pair(d):
        first = y_at(d) * TILES
        mine = grad[pl.ds(core * (HALF // 16) + first, TILES)].astype(jnp.float32)
        return mine + g_core[pl.ds(first, TILES)].astype(jnp.float32)

    def g_go(d):
        g_send[d] = g_pair(d).astype(jnp.bfloat16)
        g_y_copy(d).start()

    loop(1, NEAR, lambda d: near_copy(d).start())
    near[group] = stats[...]
    qt[...] = query.astype(jnp.float32).T.astype(jnp.bfloat16)
    qint[...] = qin[...].astype(jnp.float32).T.astype(jnp.bfloat16)
    pu[...] = raised.T.astype(jnp.bfloat16)
    minus = jnp.where(owned, -1.0, 0.0).astype(jnp.bfloat16)
    both = jnp.concatenate([raised.astype(jnp.bfloat16), minus], axis=1)
    sides[...] = jnp.dot(pt[...], both, preferred_element_type=jnp.float32)
    pgt[...] = lax.dot_general(qt[...], minus, NT, preferred_element_type=jnp.float32)
    word = lax.broadcasted_iota(jnp.int32, (K, SLOT_DEV), 0).astype(jnp.float32)
    word = word.astype(jnp.bfloat16)
    onto_range(0, 12)
    loop(1, NEAR, lambda d: near_copy(d).wait_recv())
    near_peak, near_total, near_positive = merge(near[...])
    mid[...] = jnp.concatenate([near_peak, near_total, near_positive, pad], axis=0)
    loop(0, nz - 1, lambda e: far_copy(e).start())
    far[z] = mid[...]

    tiles = (D // 16, 16, Q_DEV)
    soft = sides[:, :Q_DEV] * jnp.exp(peak - near_peak)
    grad[:, 0] = soft.astype(jnp.bfloat16).reshape(tiles)
    grad[:, 1] = sides[:, Q_DEV:].astype(jnp.bfloat16).reshape(tiles)
    g_core_copy().start()
    loop(1, NX, lambda d: q_copy(d).start())
    q_all[x] = qint[pl.ds(pl.multiple_of(x * HEAD_ROWS, 16), HEAD_ROWS), :]
    onto_range(12, 24)
    g_core_copy().wait_recv()
    loop(1, NY, g_go)
    onto_range(24, 72)

    def g_part(t):
        return (pl.ds(t * G_TILE, G_TILE), slice(None))

    def g_owner(t):
        return (t * nz) // TILES

    def g_place(t):
        return sum(1 for s in range(t) if g_owner(s) == g_owner(t))

    def z_copy(t):
        p = g_place(t)
        return copy(g_sum.at[t], g_z.at[p, z], gz_send.at[t], gz_recv.at[p, z], along(g_owner(t)))

    def z_heard(t, o):
        p = g_place(t)
        return copy(g_z.at[p, o], g_z.at[p, o], gz_send.at[t], gz_recv.at[p, o], along(o))

    g_final = g_fin.at[x, core, y]

    def back_copy(t, e):
        to = along(lax.rem(z + hop(e), nz))
        return copy(g_red.at[g_place(t)], g_final.at[g_part(t)], gr_send.at[g_place(t), e], gr_recv.at[t], to)

    loop(1, NY, lambda d: g_y_copy(d).wait_recv())
    g_total = g_pair(0)
    for d in range(1, NY):
        g_total = g_total + g_block[d].astype(jnp.float32)
    g_sum[...] = g_total.astype(jnp.bfloat16)
    for t in range(TILES):

        @pl.when(z == g_owner(t))
        def _(t=t):
            g_z[g_place(t), z] = g_sum[t]

        @pl.when(z != g_owner(t))
        def _(t=t):
            z_copy(t).start()

    onto_range(72, M)
    loop(0, nz - 1, lambda e: far_copy(e).wait_recv())
    last_peak, total, positive = merge(far[...])
    log_total = last_peak + jnp.log(total)
    loss[...] = log_total - positive
    loss_out = pltpu.make_async_copy(loss, loss_hbm, out_sems.at[0])
    loss_out.start()
    scaled[...] = qt[...].astype(jnp.float32) * jnp.exp(peak - log_total)

    def split(m):
        part = scaled[pl.ds(pl.multiple_of(m * SUB, SUB), SUB), :]
        upper = part.astype(jnp.bfloat16)
        lower = (part - upper.astype(jnp.float32)).astype(jnp.bfloat16)
        return jnp.concatenate([upper, lower], axis=0)

    def mass_of(m):
        return mass[pl.ds(pl.multiple_of(m * Q_DEV, Q_DEV), Q_DEV), :]

    def x_at(a, sign=1):
        return lax.rem(x + 4 + sign * spread(a), NX)

    def c_compute(a):
        for i in range(NY * C_SUBS):
            m0 = other * (M // 2) + x_at(a) * (NY * C_SUBS) + i
            m1 = core * (M // 2) + x_at(a) * (NY * C_SUBS) + i
            nil = jnp.zeros((2 * SUB, Q_DEV), jnp.bfloat16)
            first = jnp.concatenate([split(m0), nil], axis=1)
            second = jnp.concatenate([nil, split(m1)], axis=1)
            sums = jnp.dot(
                jnp.concatenate([first, second], axis=0),
                jnp.concatenate([mass_of(m0), mass_of(m1)], axis=0),
                preferred_element_type=jnp.float32,
            )
            for at, m in ((0, m0), (2 * SUB, m1)):
                rows = pl.ds(pl.multiple_of(m * SUB, SUB), SUB)
                book[rows, :] = sums[at : at + SUB] + sums[at + SUB : at + 2 * SUB] + fixed[rows, :]
        c_core_copy(a).start()

    def c_core_copy(a):
        rows = pl.ds(pl.multiple_of(other * HALF + x_at(a) * NY * C_ROWS, 8), NY * C_ROWS)
        return copy(book.at[rows], c_core.at[a], cc_sems.at[0, a], cc_sems.at[1, a], sibling)

    def c_chip_copy(s):
        return copy(c_send.at[s], c_block.at[s], cy_sems.at[0, s], cy_sems.at[1, s], chip(s))

    def c_add(s):
        to_x, to_y = chip_at(s, 1)
        rows = pl.ds(pl.multiple_of(core * HALF + (to_x * NY + to_y) * C_ROWS, 8), C_ROWS)
        there = pl.ds(pl.multiple_of(to_y * C_ROWS, 8), C_ROWS)
        c_send[s] = book[rows, :] + c_core[s // NY, there, :]

    def c_go(s):
        c_add(s)
        c_chip_copy(s).start()

    def c_forward(a, count):
        c_core_copy(a).wait_recv()
        loop(a * NY, a * NY + count, c_go)

    def c_both(a):
        c_compute(a)
        c_forward(a - 1, NY)

    c_compute(0)
    loop(1, NX, c_both)
    c_forward(NX - 1, NY - 1)
    c_add(CHIPS - 1)

    for t in range(TILES):

        @pl.when(z == g_owner(t))
        def _(t=t):
            loop(0, nz - 1, lambda e: z_heard(t, lax.rem(z + hop(e), nz)).wait_recv())
            weights = jnp.exp(far[...][:, 0, :] - log_total)
            whole = jnp.zeros((16, Q_DEV), jnp.float32)
            for o in range(nz):
                whole = whole + g_z[g_place(t), o, 0].astype(jnp.float32) * weights[o : o + 1, :]
                whole = whole + g_z[g_place(t), o, 1].astype(jnp.float32)
            g_red[g_place(t)] = whole.astype(jnp.bfloat16)
            loop(0, nz - 1, lambda e: back_copy(t, e).start())
            g_final[g_part(t)] = whole.astype(jnp.bfloat16)

    def interleave(tile):
        down = lax.broadcasted_iota(jnp.int32, (SUB, LANES), 0)
        across = lax.broadcasted_iota(jnp.int32, (SUB, LANES), 1)
        index = down * (LANES // SUB) + across // SUB
        mixed = jnp.zeros((SUB, LANES), jnp.float32)
        for j in range(SUB):
            row = jnp.broadcast_to(tile[j : j + 1, :], (SUB, LANES))
            row = jnp.take_along_axis(row, index, axis=1, mode="promise_in_bounds")
            mixed = jnp.where(across % SUB == j, row, mixed)
        return mixed

    loop(0, CHIPS - 1, lambda s: c_chip_copy(s).wait_recv())
    c_total = c_send[CHIPS - 1]
    for s in range(CHIPS - 1):
        c_total = c_total + c_block[s]
    for i in range(C_SUBS):
        for part in range(2):
            tile = c_total[i * SUB : (i + 1) * SUB, part * LANES : (part + 1) * LANES]
            c_sum[pl.ds((2 * i + part) * SUB, SUB), :] = tile

    odd, pair, pairs = lax.rem(z, 2), z // 2, nz // 2
    mate = along(z + 1 - 2 * odd)

    def half_at(which):
        return pl.ds(pl.multiple_of(which * C_ROWS, 8), C_ROWS)

    def c_pair_copy():
        return copy(c_sum.at[half_at(1 - odd)], c_pair, cp_sems.at[0], cp_sems.at[1], mate)

    def c_many_copy(e):
        to = along(lax.rem(pair + hop(e, pairs), pairs) * 2 + odd)
        return copy(c_half, c_many.at[pair], cz_sems.at[0, e], cz_sems.at[1, e], to)

    c_pair_copy().start()

    def c_final_at(side, place):
        return c_fin.at[pl.ds(pl.multiple_of((side * CHIPS + place) * 2 * C_ROWS, 8), 2 * C_ROWS)]

    c_final = c_final_at(core, x * NY + y)
    def g_at(side, s):
        from_x, from_y = chip_at(s, -1)
        return g_fin.at[from_x, side, from_y]

    def g_out(s):
        return copy(g_final, g_final, gf_sems.at[0, s], gf_sems.at[1, s], chip(s))

    def g_in(s):
        return copy(g_at(core, s), g_at(core, s), gf_sems.at[0, s], gf_sems.at[1, s], chip(s))

    def g_row(side, a):
        return g_fin.at[x_at(a, -1), side]

    def g_share(a):
        return copy(g_row(core, a), g_row(core, a), gs_sems.at[0, a], gs_sems.at[1, a], sibling)

    def g_shared(a):
        return copy(g_row(other, a), g_row(other, a), gs_sems.at[0, a], gs_sems.at[1, a], sibling)

    def c_out(s):
        return copy(c_final, c_final, cf_sems.at[0, s], cf_sems.at[1, s], chip(s))

    def c_at(side, s):
        return c_final_at(side, place_at(s, -1))

    def c_in(s):
        return copy(c_at(core, s), c_at(core, s), cf_sems.at[0, s], cf_sems.at[1, s], chip(s))

    def c_row(side, a):
        first = (side * CHIPS + x_at(a, -1) * NY) * 2 * C_ROWS
        return c_fin.at[pl.ds(pl.multiple_of(first, 8), NY * 2 * C_ROWS)]

    def c_share(a):
        return copy(c_row(core, a), c_row(core, a), cs_sems.at[0, a], cs_sems.at[1, a], sibling)

    def c_shared(a):
        return copy(c_row(other, a), c_row(other, a), cs_sems.at[0, a], cs_sems.at[1, a], sibling)

    c_pair_copy().wait_recv()
    c_kept = c_sum[half_at(odd), :] + c_pair[...]
    c_half[...] = c_kept
    c_many[pair] = c_kept
    loop(0, pairs - 1, lambda e: c_many_copy(e).start())
    for t in range(TILES):

        @pl.when(z != g_owner(t))
        def _(t=t):
            back_copy(t, 0).wait_recv()

    loop(0, CHIPS - 1, lambda s: g_out(s).start())
    loop(0, pairs - 1, lambda e: c_many_copy(e).wait_recv())
    c_total = c_many[0]
    for o in range(1, pairs):
        c_total = c_total + c_many[o]
    first = pl.multiple_of(odd * C_ROWS, 8)
    for i in range(C_SUBS):
        c_final[pl.ds(pl.multiple_of(first + i * SUB, 8), SUB), :] = interleave(
            c_total[i * SUB : (i + 1) * SUB]
        )

    def c_back_copy():
        return copy(c_final.at[half_at(odd)], c_final.at[half_at(odd)], cb_sems.at[0], cb_sems.at[1], mate)

    c_back_copy().start()
    c_back_copy().wait_recv()
    loop(0, CHIPS - 1, lambda s: c_out(s).start())

    def pass_on(came, share):
        def act(a):
            loop(a * NY, lax.min(a * NY + NY, CHIPS - 1), lambda s: came(s).wait_recv())
            share(a).start()

        loop(0, NX, act)

    pass_on(g_in, g_share)
    loop(1, NX, lambda d: q_copy(d).wait_recv())
    loop(0, NX, lambda a: g_shared(a).wait_recv())
    total = jnp.zeros((HEAD_ROWS, D), jnp.float32)
    for o in range(NX):
        total = total + lax.dot_general(
            q_all[o], g_fin[o].reshape(D, Q_DEV), NT, preferred_element_type=jnp.float32
        )
    head[...] = total
    head_out = pltpu.make_async_copy(head, head_hbm, out_sems.at[1])
    head_out.start()
    pass_on(c_in, c_share)
    loop(0, NX, lambda a: c_shared(a).wait_recv())
    for u in range(2 * SUB):
        out[:, u * LANES : (u + 1) * LANES] = c_fin[pl.ds(u, M, stride=2 * SUB), :]
    book_out = pltpu.make_async_copy(out, out_hbm, out_sems.at[2])
    book_out.start()

    loop(1, NEAR, lambda d: near_copy(d).wait_send())
    loop(0, nz - 1, lambda e: far_copy(e).wait_send())
    loop(1, NX, lambda d: q_copy(d).wait_send())
    g_core_copy().wait_send()
    loop(0, NX, lambda a: c_core_copy(a).wait_send())
    loop(1, NY, lambda d: g_y_copy(d).wait_send())
    loop(0, CHIPS - 1, lambda s: c_chip_copy(s).wait_send())
    for t in range(TILES):

        @pl.when(z == g_owner(t))
        def _(t=t):
            loop(0, nz - 1, lambda e: back_copy(t, e).wait_send())

        @pl.when(z != g_owner(t))
        def _(t=t):
            z_copy(t).wait_send()

    c_pair_copy().wait_send()
    loop(0, pairs - 1, lambda e: c_many_copy(e).wait_send())
    c_back_copy().wait_send()
    loop(0, CHIPS - 1, lambda s: g_out(s).wait_send())
    loop(0, NX, lambda a: g_share(a).wait_send())
    loop(0, CHIPS - 1, lambda s: c_out(s).wait_send())
    loop(0, NX, lambda a: c_share(a).wait_send())
    loss_out.wait()
    head_out.wait()
    book_out.wait()


def finish_kernel(loss_in, head_in, book_in, loss_out, head_out, book_out, loss, head, book, sems):
    moves = [(loss_in, loss, loss_out)]
    for i in range(2):
        rows = pl.ds(i * (HEAD_ROWS // 2), HEAD_ROWS // 2)
        moves.append((head_in.at[rows], head.at[rows], head_out.at[rows]))
    for i in range(3):
        rows = pl.ds(i * (M // 3), M // 3)
        moves.append((book_in.at[rows], book.at[rows], book_out.at[rows]))
    ins = [pltpu.make_async_copy(src, mid, sems.at[0, i]) for i, (src, mid, _) in enumerate(moves)]
    outs = [pltpu.make_async_copy(mid, dst, sems.at[1, i]) for i, (_, mid, dst) in enumerate(moves)]
    for each in ins:
        each.start()
    for one, two in zip(ins, outs):
        one.wait()
        two.start()
    for each in outs:
        each.wait()


def step(nz, queries_in, head_weight, codebook, codes, slab_sizes, positive_ids):
    left = pl.BlockSpec(memory_space=pltpu.HBM)
    dma = pltpu.SemaphoreType.DMA
    f32, bf16 = jnp.float32, jnp.bfloat16
    per = -(-TILES // nz)
    loss, head_grad, book = pl.pallas_call(
        functools.partial(step_kernel, nz),
        out_shape=[
            jax.ShapeDtypeStruct((1, Q_DEV), f32),
            jax.ShapeDtypeStruct((HEAD_ROWS, D), f32),
            jax.ShapeDtypeStruct((M, K * SUB), f32),
        ],
        in_specs=[pl.BlockSpec(memory_space=pltpu.SMEM)] + [left] * 5,
        out_specs=[left] * 3,
        scratch_shapes=[
            pltpu.VMEM((1, Q_DEV), jnp.int32),
            pltpu.VMEM((Q_DEV, D), bf16),
            pltpu.VMEM((D, D), bf16),
            pltpu.VMEM((M, K * SUB), bf16),
            pltpu.VMEM((M, SLOT_DEV), jnp.int32),
            pltpu.VMEM((2 * D, LANES), f32),
            pltpu.VMEM((D, SLOT_DEV), bf16),
            pltpu.VMEM((D, Q_DEV), bf16),
            pltpu.VMEM((D, Q_DEV), bf16),
            pltpu.VMEM((D, SLOT_DEV), f32),
            pltpu.VMEM((8, Q_DEV), f32),
            pltpu.VMEM((NEAR, 8, Q_DEV), f32),
            pltpu.VMEM((nz, 8, Q_DEV), f32),
            pltpu.VMEM((8, Q_DEV), f32),
            pltpu.VMEM((D, K), f32),
            pltpu.VMEM((Q_DEV, SLOT_DEV), bf16),
            pltpu.VMEM((D, 2 * Q_DEV), f32),
            pltpu.VMEM((M * Q_DEV, K), bf16),
            pltpu.VMEM((D, K), f32),
            pltpu.VMEM((D, Q_DEV), f32),
            pltpu.VMEM((1, Q_DEV), f32),
            pltpu.VMEM((HEAD_ROWS, D), f32),
            pltpu.VMEM((M, K * SUB), f32),
            pltpu.VMEM((NX, HEAD_ROWS, Q_DEV), bf16),
            pltpu.VMEM((D // 16, 2, 16, Q_DEV), bf16),
            pltpu.VMEM((HALF // 16, 2, 16, Q_DEV), bf16),
            pltpu.VMEM((NY, TILES, 2, 16, Q_DEV), bf16),
            pltpu.VMEM((NY, TILES, 2, 16, Q_DEV), bf16),
            pltpu.VMEM((TILES, 2, 16, Q_DEV), bf16),
            pltpu.VMEM((per, nz, 2, 16, Q_DEV), bf16),
            pltpu.VMEM((per, 16, Q_DEV), bf16),
            pltpu.VMEM((NX, 2, NY, G_ROWS, Q_DEV), bf16),
            pltpu.VMEM((NX, NY * C_ROWS, K), f32),
            pltpu.VMEM((CHIPS, C_ROWS, K), f32),
            pltpu.VMEM((CHIPS, C_ROWS, K), f32),
            pltpu.VMEM((2 * C_ROWS, LANES), f32),
            pltpu.VMEM((C_ROWS, LANES), f32),
            pltpu.VMEM((C_ROWS, LANES), f32),
            pltpu.VMEM((nz // 2, C_ROWS, LANES), f32),
            pltpu.VMEM((2 * D, LANES), f32),
            dma((5,)),
            dma((3,)),
            dma((2, NEAR)),
            dma((2, nz)),
            dma((2, NX)),
            dma((2,)),
            dma((2, NY)),
            dma((TILES,)),
            dma((per, nz)),
            dma((per, nz)),
            dma((TILES,)),
            dma((2, CHIPS)),
            dma((2, NX)),
            dma((2, NX)),
            dma((2, CHIPS)),
            dma((2,)),
            dma((2, nz // 2)),
            dma((2,)),
            dma((2, CHIPS)),
            dma((2, NX)),
        ],
        compiler_params=pltpu.CompilerParams(
            collective_id=0, has_side_effects=True, vmem_limit_bytes=VMEM_BYTES
        ),
    )(slab_sizes, positive_ids.reshape(1, Q_DEV), queries_in, head_weight, codebook, codes.T)
    outs = [(1, Q_DEV), (HEAD_ROWS, D), (M, K * SUB)]
    loss, head_grad, book = pl.pallas_call(
        finish_kernel,
        out_shape=[jax.ShapeDtypeStruct(shape, f32) for shape in outs],
        in_specs=[left] * 3,
        out_specs=[left] * 3,
        scratch_shapes=[pltpu.VMEM(shape, f32) for shape in outs] + [dma((2, 6))],
        compiler_params=pltpu.CompilerParams(vmem_limit_bytes=VMEM_BYTES),
    )(loss, head_grad, book)
    return loss.reshape(Q_DEV), head_grad, book


def solution(mesh):
    nz = mesh.shape["corpus"] // (2 * NY)
    return jax.shard_map(
        functools.partial(step, nz),
        mesh=mesh,
        in_specs=(P("query", None), P(), P(), P("corpus", None), P("corpus"), P("query")),
        out_specs=(P("query"), P("query", None), P()),
        check_vma=False,
    )
```

time: 75.8 us -> 67.1 us (0.89)
  Pallas kernels: 70.3 us -> 65.6 us
  local copies, waits for them, and re-layouts: 3.96 us -> 0 us
    pallas_call x1, Pallas kernels: 70.3 us -> 63.5 us  [step(): pl.pallas_call(functools.partial(step_kernel, nz), out_shape=[jax.ShapeDt...]
    unnamed x5 -> x0, local copies, waits for them, and re-layouts: 3.96 us -> none
    pallas_call x0 -> x1, Pallas kernels: none -> 2.14 us  [step(): pl.pallas_call(finish_kernel, out_shape=[jax.ShapeDtypeStruct(shape, f32)...]
where the time goes in v3:
time: 67.1 us; the launch traced here: 66.9 us
  Pallas kernels  65.6 us (98%)
  between operations  1.29 us (2%)
    pallas_call x1, Pallas kernels, step(): pl.pallas_call(functools.partial(step_kernel, nz), out_shape=[jax.ShapeDt...  63.5 us
    pallas_call x1, Pallas kernels, step(): pl.pallas_call(finish_kernel, out_shape=[jax.ShapeDtypeStruct(shape, f32)...  2.14 us

profile of v3, /device:TPU:1, one launch (start us, length us, event | category | flops | bytes accessed | tf_op | source)
XLA Modules:
  0.0 66.9 jit_solution(16863520652632350312)
XLA Ops:
  1.3 63.5 %shard_map.85 = (f32[1,128]{1,0:T(1,128)}, f32[192,768]{1,0:T(8,128)}, f32[96,2048]{1,0:T(8,128)}) custom-call(s32[1]{0:T(128)S(6)} %copy.9.length_ref, s32[1,128]{1,0:T(1,128)} %bitcast.4, bf16[128,768]{1,0:T(8,128)(2,1)} %qin_hbm.1, bf16[768,768]{1,0:T(8,128)(2,1)} %weight_hbm.1, bf16[96,2048]{1,0:T(8,128)(2,1)} %codebook_hbm.1, s32[96,384]{1,0:T(8,128)} %bitcast.3), custom_call_target="tpu_custom_call" | custom-call | tf_op jit(solution)/shard_map/pallas_call | solution.py:554
  64.8 2.1 %shard_map.86 = (f32[1,128]{1,0:T(1,128)}, f32[192,768]{1,0:T(8,128)}, f32[96,2048]{1,0:T(8,128)}) custom-call(f32[1,128]{1,0:T(1,128)} %get-tuple-element.9.loss_in, f32[192,768]{1,0:T(8,128)} %get-tuple-element.10.head_in, f32[96,2048]{1,0:T(8,128)} %get-tuple-element.11.book_in), custom_call_target="tpu_custom_call" | custom-call | tf_op jit(solution)/shard_map/pallas_call | solution.py:630

commit v4 on v3

--- a/solution.py
+++ b/solution.py
@@ -27,7 +27,7 @@
 NEAR = 2 * NY
 MESH = pl.DeviceIdType.MESH
 NT = (((1,), (1,)), ((), ()))
-VMEM_BYTES = 64 * 1024 * 1024 - 65536
+VMEM_BYTES = 48 * 1024 * 1024
 
 
 def loop(start, count, act):
@@ -45,14 +45,14 @@
 def step_kernel(
     nz,
     length_ref, ids_hbm, qin_hbm, weight_hbm, codebook_hbm, codes_hbm,
-    loss_hbm, head_hbm, out_hbm,
+    loss, head, out,
     ids, qin, weight, codebook, codes, table, pt, qt, qint, pgt, stats, near, far, mid, book,
-    pu, sides, mass, fixed, scaled, loss, head, out,
+    pu, sides, mass, fixed, scaled,
     q_all, grad, g_core, g_send, g_block, g_sum, g_z, g_red, g_fin,
-    c_core, c_send, c_block, c_sum, c_pair, c_half, c_many, c_fin,
-    in_sems, out_sems, near_sems, far_sems,
+    c_core, c_send, c_block, c_half, c_many, c_fin,
+    in_sems, near_sems, far_sems,
     q_sems, gc_sems, gy_sems, gz_send, gz_recv, gr_send, gr_recv, gf_sems, gs_sems,
-    cc_sems, cy_sems, cp_sems, cz_sems, cb_sems, cf_sems, cs_sems,
+    cc_sems, cy_sems, cz_sems, cf_sems, cs_sems,
 ):
     me = lax.axis_index("corpus")
     x, y, z, core = lax.axis_index("query"), me // (2 * nz), lax.rem(me // 2, nz), lax.rem(me, 2)
@@ -85,6 +85,15 @@
     def chip(s, sign=1):
         to_x, to_y = chip_at(s, sign)
         return device(to_x, to_y, z, core)
+
+    odd, pair, pairs = lax.rem(z, 2), z // 2, nz // 2
+
+    def chip_beside(s):
+        to_x, to_y = chip_at(s, 1)
+        return device(to_x, to_y, z + 1 - 2 * odd, core)
+
+    def half_at(which):
+        return pl.ds(pl.multiple_of(which * C_ROWS, 8), C_ROWS)
 
     def y_at(d):
         return lax.rem(y + d, NY)
@@ -110,6 +119,7 @@
         load.start()
     loop(1, NEAR, lambda d: greet(around(lax.rem(group + d, NEAR))))
     loop(0, 12, lambda s: greet(chip(s)))
+    loop(0, CHIPS - 1, lambda s: greet(chip_beside(s)))
 
     wide = K * SUB // 2
     down = lax.broadcasted_iota(jnp.int32, (wide, wide), 0)
@@ -160,7 +170,7 @@
     positive = jnp.sum(jnp.where(owned, scores, 0.0), axis=0, keepdims=True)
     pad = jnp.zeros((5, Q_DEV), jnp.float32)
     stats[...] = jnp.concatenate([peak, total, positive, pad], axis=0)
-    pl.semaphore_wait(barrier, NEAR - 1 + nz - 1 + 12)
+    pl.semaphore_wait(barrier, NEAR - 1 + nz - 1 + 12 + CHIPS - 1)
 
     def merge(slots):
         peaks, totals, positives = slots[:, 0, :], slots[:, 1, :], slots[:, 2, :]
@@ -290,8 +300,6 @@
     last_peak, total, positive = merge(far[...])
     log_total = last_peak + jnp.log(total)
     loss[...] = log_total - positive
-    loss_out = pltpu.make_async_copy(loss, loss_hbm, out_sems.at[0])
-    loss_out.start()
     scaled[...] = qt[...].astype(jnp.float32) * jnp.exp(peak - log_total)
 
     def split(m):
@@ -300,58 +308,67 @@
         lower = (part - upper.astype(jnp.float32)).astype(jnp.bfloat16)
         return jnp.concatenate([upper, lower], axis=0)
 
-    def mass_of(m):
-        return mass[pl.ds(pl.multiple_of(m * Q_DEV, Q_DEV), Q_DEV), :]
-
     def x_at(a, sign=1):
         return lax.rem(x + 4 + sign * spread(a), NX)
 
-    def c_compute(a):
-        for i in range(NY * C_SUBS):
-            m0 = other * (M // 2) + x_at(a) * (NY * C_SUBS) + i
-            m1 = core * (M // 2) + x_at(a) * (NY * C_SUBS) + i
+    def c_compute(side, a):
+        for i in range(0, NY * C_SUBS, 2):
+            m = side * (M // 2) + x_at(a) * (NY * C_SUBS) + i
             nil = jnp.zeros((2 * SUB, Q_DEV), jnp.bfloat16)
-            first = jnp.concatenate([split(m0), nil], axis=1)
-            second = jnp.concatenate([nil, split(m1)], axis=1)
+            first = jnp.concatenate([split(m), nil], axis=1)
+            second = jnp.concatenate([nil, split(m + 1)], axis=1)
+            both_of = mass[pl.ds(pl.multiple_of(m * Q_DEV, Q_DEV), 2 * Q_DEV), :]
             sums = jnp.dot(
-                jnp.concatenate([first, second], axis=0),
-                jnp.concatenate([mass_of(m0), mass_of(m1)], axis=0),
-                preferred_element_type=jnp.float32,
+                jnp.concatenate([first, second], axis=0), both_of, preferred_element_type=jnp.float32
             )
-            for at, m in ((0, m0), (2 * SUB, m1)):
-                rows = pl.ds(pl.multiple_of(m * SUB, SUB), SUB)
-                book[rows, :] = sums[at : at + SUB] + sums[at + SUB : at + 2 * SUB] + fixed[rows, :]
-        c_core_copy(a).start()
+            rows = pl.ds(pl.multiple_of(m * SUB, SUB), 2 * SUB)
+            sums = [sums[k * SUB : (k + 1) * SUB] for k in range(4)]
+            book[rows, :] = jnp.concatenate([sums[0] + sums[1], sums[2] + sums[3]], axis=0) + fixed[rows, :]
 
     def c_core_copy(a):
         rows = pl.ds(pl.multiple_of(other * HALF + x_at(a) * NY * C_ROWS, 8), NY * C_ROWS)
         return copy(book.at[rows], c_core.at[a], cc_sems.at[0, a], cc_sems.at[1, a], sibling)
 
     def c_chip_copy(s):
-        return copy(c_send.at[s], c_block.at[s], cy_sems.at[0, s], cy_sems.at[1, s], chip(s))
+        return copy(
+            c_send.at[s, half_at(odd)], c_block.at[s], cy_sems.at[0, s], cy_sems.at[1, s], chip(s)
+        )
+
+    def c_beside_copy(s):
+        k = CHIPS + s
+        return copy(
+            c_send.at[s, half_at(1 - odd)], c_block.at[k], cy_sems.at[0, k], cy_sems.at[1, k], chip_beside(s)
+        )
 
     def c_add(s):
         to_x, to_y = chip_at(s, 1)
         rows = pl.ds(pl.multiple_of(core * HALF + (to_x * NY + to_y) * C_ROWS, 8), C_ROWS)
         there = pl.ds(pl.multiple_of(to_y * C_ROWS, 8), C_ROWS)
-        c_send[s] = book[rows, :] + c_core[s // NY, there, :]
+        both = book[rows, :] + c_core[s // NY, there, :]
+        for i in range(C_SUBS):
+            for part in range(2):
+                tile = both[i * SUB : (i + 1) * SUB, part * LANES : (part + 1) * LANES]
+                c_send[s, pl.ds((2 * i + part) * SUB, SUB), :] = tile
 
     def c_go(s):
         c_add(s)
+        c_beside_copy(s).start()
         c_chip_copy(s).start()
 
-    def c_forward(a, count):
+    def c_near(a):
+        c_compute(other, a)
+        c_core_copy(a).start()
+
+    def c_away(a, count):
+        c_compute(core, a)
         c_core_copy(a).wait_recv()
         loop(a * NY, a * NY + count, c_go)
 
-    def c_both(a):
-        c_compute(a)
-        c_forward(a - 1, NY)
-
-    c_compute(0)
-    loop(1, NX, c_both)
-    c_forward(NX - 1, NY - 1)
+    loop(0, NX, c_near)
+    loop(0, NX - 1, lambda a: c_away(a, NY))
+    c_away(NX - 1, NY - 1)
     c_add(CHIPS - 1)
+    c_beside_copy(CHIPS - 1).start()
 
     for t in range(TILES):
 
@@ -379,28 +396,19 @@
         return mixed
 
     loop(0, CHIPS - 1, lambda s: c_chip_copy(s).wait_recv())
-    c_total = c_send[CHIPS - 1]
-    for s in range(CHIPS - 1):
-        c_total = c_total + c_block[s]
-    for i in range(C_SUBS):
-        for part in range(2):
-            tile = c_total[i * SUB : (i + 1) * SUB, part * LANES : (part + 1) * LANES]
-            c_sum[pl.ds((2 * i + part) * SUB, SUB), :] = tile
-
-    odd, pair, pairs = lax.rem(z, 2), z // 2, nz // 2
-    mate = along(z + 1 - 2 * odd)
-
-    def half_at(which):
-        return pl.ds(pl.multiple_of(which * C_ROWS, 8), C_ROWS)
-
-    def c_pair_copy():
-        return copy(c_sum.at[half_at(1 - odd)], c_pair, cp_sems.at[0], cp_sems.at[1], mate)
+    loop(0, CHIPS, lambda s: c_beside_copy(s).wait_recv())
+    c_total = c_send[CHIPS - 1, half_at(odd), :]
+    for s in range(2 * CHIPS):
+        if s != CHIPS - 1:
+            c_total = c_total + c_block[s]
 
     def c_many_copy(e):
         to = along(lax.rem(pair + hop(e, pairs), pairs) * 2 + odd)
         return copy(c_half, c_many.at[pair], cz_sems.at[0, e], cz_sems.at[1, e], to)
 
-    c_pair_copy().start()
+    c_half[...] = c_total
+    c_many[pair] = c_total
+    loop(0, pairs - 1, lambda e: c_many_copy(e).start())
 
     def c_final_at(side, place):
         return c_fin.at[pl.ds(pl.multiple_of((side * CHIPS + place) * 2 * C_ROWS, 8), 2 * C_ROWS)]
@@ -426,13 +434,23 @@
         return copy(g_row(other, a), g_row(other, a), gs_sems.at[0, a], gs_sems.at[1, a], sibling)
 
     def c_out(s):
-        return copy(c_final, c_final, cf_sems.at[0, s], cf_sems.at[1, s], chip(s))
+        mine = c_final.at[half_at(odd)]
+        return copy(mine, mine, cf_sems.at[0, s], cf_sems.at[1, s], chip(s))
+
+    def c_out_beside(s):
+        mine = c_final.at[half_at(odd)]
+        return copy(mine, mine, cf_sems.at[0, CHIPS + s], cf_sems.at[1, CHIPS + s], chip_beside(s))
 
     def c_at(side, s):
         return c_final_at(side, place_at(s, -1))
 
     def c_in(s):
-        return copy(c_at(core, s), c_at(core, s), cf_sems.at[0, s], cf_sems.at[1, s], chip(s))
+        came = c_at(core, s).at[half_at(odd)]
+        return copy(came, came, cf_sems.at[0, s], cf_sems.at[1, s], chip(s))
+
+    def c_in_beside(s):
+        came = c_at(core, s).at[half_at(1 - odd)]
+        return copy(came, came, cf_sems.at[0, CHIPS + s], cf_sems.at[1, CHIPS + s], chip(s))
 
     def c_row(side, a):
         first = (side * CHIPS + x_at(a, -1) * NY) * 2 * C_ROWS
@@ -444,11 +462,6 @@
     def c_shared(a):
         return copy(c_row(other, a), c_row(other, a), cs_sems.at[0, a], cs_sems.at[1, a], sibling)
 
-    c_pair_copy().wait_recv()
-    c_kept = c_sum[half_at(odd), :] + c_pair[...]
-    c_half[...] = c_kept
-    c_many[pair] = c_kept
-    loop(0, pairs - 1, lambda e: c_many_copy(e).start())
     for t in range(TILES):
 
         @pl.when(z != g_owner(t))
@@ -466,12 +479,13 @@
             c_total[i * SUB : (i + 1) * SUB]
         )
 
-    def c_back_copy():
-        return copy(c_final.at[half_at(odd)], c_final.at[half_at(odd)], cb_sems.at[0], cb_sems.at[1], mate)
-
-    c_back_copy().start()
-    c_back_copy().wait_recv()
-    loop(0, CHIPS - 1, lambda s: c_out(s).start())
+
+    def c_spread(s):
+        c_out_beside(s).start()
+        c_out(s).start()
+
+    loop(0, CHIPS - 1, c_spread)
+    c_out_beside(CHIPS - 1).start()
 
     def pass_on(came, share):
         def act(a):
@@ -489,14 +503,16 @@
             q_all[o], g_fin[o].reshape(D, Q_DEV), NT, preferred_element_type=jnp.float32
         )
     head[...] = total
-    head_out = pltpu.make_async_copy(head, head_hbm, out_sems.at[1])
-    head_out.start()
-    pass_on(c_in, c_share)
+
+    def c_pass(a):
+        loop(a * NY, lax.min(a * NY + NY, CHIPS - 1), lambda s: c_in(s).wait_recv())
+        loop(a * NY, a * NY + NY, lambda s: c_in_beside(s).wait_recv())
+        c_share(a).start()
+
+    loop(0, NX, c_pass)
     loop(0, NX, lambda a: c_shared(a).wait_recv())
     for u in range(2 * SUB):
         out[:, u * LANES : (u + 1) * LANES] = c_fin[pl.ds(u, M, stride=2 * SUB), :]
-    book_out = pltpu.make_async_copy(out, out_hbm, out_sems.at[2])
-    book_out.start()
 
     loop(1, NEAR, lambda d: near_copy(d).wait_send())
     loop(0, nz - 1, lambda e: far_copy(e).wait_send())
@@ -515,51 +531,44 @@
         def _(t=t):
             z_copy(t).wait_send()
 
-    c_pair_copy().wait_send()
+    loop(0, CHIPS, lambda s: c_beside_copy(s).wait_send())
     loop(0, pairs - 1, lambda e: c_many_copy(e).wait_send())
-    c_back_copy().wait_send()
     loop(0, CHIPS - 1, lambda s: g_out(s).wait_send())
     loop(0, NX, lambda a: g_share(a).wait_send())
     loop(0, CHIPS - 1, lambda s: c_out(s).wait_send())
+    loop(0, CHIPS, lambda s: c_out_beside(s).wait_send())
     loop(0, NX, lambda a: c_share(a).wait_send())
-    loss_out.wait()
-    head_out.wait()
-    book_out.wait()
-
-
-def finish_kernel(loss_in, head_in, book_in, loss_out, head_out, book_out, loss, head, book, sems):
-    moves = [(loss_in, loss, loss_out)]
+
+
+def finish_kernel(loss_in, head_in, book_in, loss_out, head_out, book_out, sems):
+    moves = [(loss_in, loss_out)]
+    for i in range(3):
+        rows = pl.ds(i * (M // 3), M // 3)
+        moves.append((book_in.at[rows], book_out.at[rows]))
     for i in range(2):
         rows = pl.ds(i * (HEAD_ROWS // 2), HEAD_ROWS // 2)
-        moves.append((head_in.at[rows], head.at[rows], head_out.at[rows]))
-    for i in range(3):
-        rows = pl.ds(i * (M // 3), M // 3)
-        moves.append((book_in.at[rows], book.at[rows], book_out.at[rows]))
-    ins = [pltpu.make_async_copy(src, mid, sems.at[0, i]) for i, (src, mid, _) in enumerate(moves)]
-    outs = [pltpu.make_async_copy(mid, dst, sems.at[1, i]) for i, (_, mid, dst) in enumerate(moves)]
-    for each in ins:
+        moves.append((head_in.at[rows], head_out.at[rows]))
+    copies = [pltpu.make_async_copy(src, dst, sems.at[i]) for i, (src, dst) in enumerate(moves)]
+    for each in copies:
         each.start()
-    for one, two in zip(ins, outs):
-        one.wait()
-        two.start()
-    for each in outs:
+    for each in copies:
         each.wait()
 
 
 def step(nz, queries_in, head_weight, codebook, codes, slab_sizes, positive_ids):
     left = pl.BlockSpec(memory_space=pltpu.HBM)
+    whole = pl.BlockSpec(memory_space=pltpu.VMEM)
     dma = pltpu.SemaphoreType.DMA
     f32, bf16 = jnp.float32, jnp.bfloat16
     per = -(-TILES // nz)
+    outs = [(1, Q_DEV), (HEAD_ROWS, D), (M, K * SUB)]
+    ins = [positive_ids.reshape(1, Q_DEV), queries_in, head_weight, codebook, codes.T]
+    ins = [pltpu.with_memory_space_constraint(each, pltpu.HBM) for each in ins]
     loss, head_grad, book = pl.pallas_call(
         functools.partial(step_kernel, nz),
-        out_shape=[
-            jax.ShapeDtypeStruct((1, Q_DEV), f32),
-            jax.ShapeDtypeStruct((HEAD_ROWS, D), f32),
-            jax.ShapeDtypeStruct((M, K * SUB), f32),
-        ],
+        out_shape=[pltpu.VMEM(shape, f32) for shape in outs],
         in_specs=[pl.BlockSpec(memory_space=pltpu.SMEM)] + [left] * 5,
-        out_specs=[left] * 3,
+        out_specs=[whole] * 3,
         scratch_shapes=[
             pltpu.VMEM((1, Q_DEV), jnp.int32),
             pltpu.VMEM((Q_DEV, D), bf16),
@@ -581,9 +590,6 @@
             pltpu.VMEM((M * Q_DEV, K), bf16),
             pltpu.VMEM((D, K), f32),
             pltpu.VMEM((D, Q_DEV), f32),
-            pltpu.VMEM((1, Q_DEV), f32),
-            pltpu.VMEM((HEAD_ROWS, D), f32),
-            pltpu.VMEM((M, K * SUB), f32),
             pltpu.VMEM((NX, HEAD_ROWS, Q_DEV), bf16),
             pltpu.VMEM((D // 16, 2, 16, Q_DEV), bf16),
             pltpu.VMEM((HALF // 16, 2, 16, Q_DEV), bf16),
@@ -594,15 +600,12 @@
             pltpu.VMEM((per, 16, Q_DEV), bf16),
             pltpu.VMEM((NX, 2, NY, G_ROWS, Q_DEV), bf16),
             pltpu.VMEM((NX, NY * C_ROWS, K), f32),
-            pltpu.VMEM((CHIPS, C_ROWS, K), f32),
-            pltpu.VMEM((CHIPS, C_ROWS, K), f32),
-            pltpu.VMEM((2 * C_ROWS, LANES), f32),
-            pltpu.VMEM((C_ROWS, LANES), f32),
+            pltpu.VMEM((CHIPS, 2 * C_ROWS, LANES), f32),
+            pltpu.VMEM((2 * CHIPS, C_ROWS, LANES), f32),
             pltpu.VMEM((C_ROWS, LANES), f32),
             pltpu.VMEM((nz // 2, C_ROWS, LANES), f32),
             pltpu.VMEM((2 * D, LANES), f32),
             dma((5,)),
-            dma((3,)),
             dma((2, NEAR)),
             dma((2, nz)),
             dma((2, NX)),
@@ -615,24 +618,21 @@
             dma((2, CHIPS)),
             dma((2, NX)),
             dma((2, NX)),
-            dma((2, CHIPS)),
-            dma((2,)),
+            dma((2, 2 * CHIPS)),
             dma((2, nz // 2)),
-            dma((2,)),
-            dma((2, CHIPS)),
+            dma((2, 2 * CHIPS)),
             dma((2, NX)),
         ],
         compiler_params=pltpu.CompilerParams(
             collective_id=0, has_side_effects=True, vmem_limit_bytes=VMEM_BYTES
         ),
-    )(slab_sizes, positive_ids.reshape(1, Q_DEV), queries_in, head_weight, codebook, codes.T)
-    outs = [(1, Q_DEV), (HEAD_ROWS, D), (M, K * SUB)]
+    )(slab_sizes, *ins)
     loss, head_grad, book = pl.pallas_call(
         finish_kernel,
         out_shape=[jax.ShapeDtypeStruct(shape, f32) for shape in outs],
-        in_specs=[left] * 3,
+        in_specs=[whole] * 3,
         out_specs=[left] * 3,
-        scratch_shapes=[pltpu.VMEM(shape, f32) for shape in outs] + [dma((2, 6))],
+        scratch_shapes=[dma((6,))],
         compiler_params=pltpu.CompilerParams(vmem_limit_bytes=VMEM_BYTES),
     )(loss, head_grad, book)
     return loss.reshape(Q_DEV), head_grad, book

time: 67.1 us -> 63.2 us (0.942)
  Pallas kernels: 65.6 us -> 61.8 us
    pallas_call x1, Pallas kernels: 63.5 us -> 60.6 us  [step(): pl.pallas_call(functools.partial(step_kernel, nz), out_shape=[pltpu.VMEM(...]
    pallas_call x1, Pallas kernels: 2.14 us -> 1.13 us  [step(): pl.pallas_call(finish_kernel, out_shape=[jax.ShapeDtypeStruct(shape, f32)...]
where the time goes in v4:
time: 63.2 us; the launch traced here: 63.1 us
  Pallas kernels  61.8 us (98%)
  between operations  1.29 us (2%)
    pallas_call x1, Pallas kernels, step(): pl.pallas_call(functools.partial(step_kernel, nz), out_shape=[pltpu.VMEM(...  60.6 us

profile of v4, /device:TPU:1, one launch (start us, length us, event | category | flops | bytes accessed | tf_op | source)
XLA Modules:
  0.0 63.1 jit_solution(6890969621695748520)
XLA Ops:
  1.3 60.6 %shard_map.85 = (f32[1,128]{1,0:T(1,128)S(1)}, f32[192,768]{1,0:T(8,128)S(1)}, f32[96,2048]{1,0:T(8,128)S(1)}) custom-call(s32[1]{0:T(128)S(6)} %copy.9.length_ref, s32[1,128]{1,0:T(1,128)} %bitcast.4, bf16[128,768]{1,0:T(8,128)(2,1)} %qin_hbm.1, bf16[768,768]{1,0:T(8,128)(2,1)} %weight_hbm.1, bf16[96,2048]{1,0:T(8,128)(2,1)} %codebook_hbm.1, s32[96,384]{1,0:T(8,128)} %bitcast.3), custom_call_target="tpu_custom_call" | custom-call | tf_op jit(solution)/shard_map/pallas_call | solution.py:567
  61.9 1.1 %shard_map.86 = (f32[1,128]{1,0:T(1,128)}, f32[192,768]{1,0:T(8,128)}, f32[96,2048]{1,0:T(8,128)}) custom-call(f32[1,128]{1,0:T(1,128)S(1)} %get-tuple-element.9.loss_in, f32[192,768]{1,0:T(8,128)S(1)} %get-tuple-element.10.head_in, f32[96,2048]{1,0:T(8,128)S(1)} %get-tuple-element.11.book_in), custom_call_target="tpu_custom_call" | custom-call | tf_op jit(solution)/shard_map/pallas_call | solution.py:630

commit v5 on v4

--- a/solution.py
+++ b/solution.py
@@ -31,6 +31,10 @@
 
 
 def loop(start, count, act):
+    if isinstance(start, int) and isinstance(count, int):
+        for step in range(start, count):
+            act(step)
+        return
     def body(step, carry):
         act(step)
         return carry
@@ -71,11 +75,11 @@
         return device(x, y, o, core)
 
     def hop(e, ring=nz):
-        return ring // 2 + ((e + 1) // 2) * (1 - 2 * lax.rem(e, 2))
+        return ring // 2 + ((e + 1) // 2) * (1 - 2 * (e % 2))
 
     def chip_at(s, sign):
         to_x = lax.rem(x + 4 + sign * spread(s // 4), NX)
-        to_y = lax.rem(y + 4 + sign * spread(lax.rem(s, 4)), NY)
+        to_y = lax.rem(y + 4 + sign * spread(s % 4), NY)
         return to_x, to_y
 
     def place_at(s, sign):
@@ -238,7 +242,7 @@
     pgt[...] = lax.dot_general(qt[...], minus, NT, preferred_element_type=jnp.float32)
     word = lax.broadcasted_iota(jnp.int32, (K, SLOT_DEV), 0).astype(jnp.float32)
     word = word.astype(jnp.bfloat16)
-    onto_range(0, 12)
+    onto_range(0, 20)
     loop(1, NEAR, lambda d: near_copy(d).wait_recv())
     near_peak, near_total, near_positive = merge(near[...])
     mid[...] = jnp.concatenate([near_peak, near_total, near_positive, pad], axis=0)
@@ -252,10 +256,10 @@
     g_core_copy().start()
     loop(1, NX, lambda d: q_copy(d).start())
     q_all[x] = qint[pl.ds(pl.multiple_of(x * HEAD_ROWS, 16), HEAD_ROWS), :]
-    onto_range(12, 24)
+    onto_range(20, 28)
     g_core_copy().wait_recv()
     loop(1, NY, g_go)
-    onto_range(24, 72)
+    onto_range(28, 72)
 
     def g_part(t):
         return (pl.ds(t * G_TILE, G_TILE), slice(None))
@@ -489,7 +493,7 @@
 
     def pass_on(came, share):
         def act(a):
-            loop(a * NY, lax.min(a * NY + NY, CHIPS - 1), lambda s: came(s).wait_recv())
+            loop(a * NY, min(a * NY + NY, CHIPS - 1), lambda s: came(s).wait_recv())
             share(a).start()
 
         loop(0, NX, act)
@@ -505,7 +509,7 @@
     head[...] = total
 
     def c_pass(a):
-        loop(a * NY, lax.min(a * NY + NY, CHIPS - 1), lambda s: c_in(s).wait_recv())
+        loop(a * NY, min(a * NY + NY, CHIPS - 1), lambda s: c_in(s).wait_recv())
         loop(a * NY, a * NY + NY, lambda s: c_in_beside(s).wait_recv())
         c_share(a).start()
 

time: 63.2 us -> 61 us (0.965)
  Pallas kernels: 61.8 us -> 59.5 us
    pallas_call x1, Pallas kernels: 60.6 us -> 58.4 us  [step(): pl.pallas_call(functools.partial(step_kernel, nz), out_shape=[pltpu.VMEM(...]
where the time goes in v5:
time: 61 us; the launch traced here: 60.8 us
  Pallas kernels  59.5 us (98%)
  between operations  1.29 us (2%)
    pallas_call x1, Pallas kernels, step(): pl.pallas_call(functools.partial(step_kernel, nz), out_shape=[pltpu.VMEM(...  58.4 us

profile of v5, /device:TPU:1, one launch (start us, length us, event | category | flops | bytes accessed | tf_op | source)
XLA Modules:
  0.0 60.8 jit_solution(6066677408683034064)
XLA Ops:
  1.3 58.4 %shard_map.85 = (f32[1,128]{1,0:T(1,128)S(1)}, f32[192,768]{1,0:T(8,128)S(1)}, f32[96,2048]{1,0:T(8,128)S(1)}) custom-call(s32[1]{0:T(128)S(6)} %copy.9.length_ref, s32[1,128]{1,0:T(1,128)} %bitcast.4, bf16[128,768]{1,0:T(8,128)(2,1)} %qin_hbm.1, bf16[768,768]{1,0:T(8,128)(2,1)} %weight_hbm.1, bf16[96,2048]{1,0:T(8,128)(2,1)} %codebook_hbm.1, s32[96,384]{1,0:T(8,128)} %bitcast.3), custom_call_target="tpu_custom_call" | custom-call | tf_op jit(solution)/shard_map/pallas_call | solution.py:571
  59.7 1.1 %shard_map.86 = (f32[1,128]{1,0:T(1,128)}, f32[192,768]{1,0:T(8,128)}, f32[96,2048]{1,0:T(8,128)}) custom-call(f32[1,128]{1,0:T(1,128)S(1)} %get-tuple-element.9.loss_in, f32[192,768]{1,0:T(8,128)S(1)} %get-tuple-element.10.head_in, f32[96,2048]{1,0:T(8,128)S(1)} %get-tuple-element.11.book_in), custom_call_target="tpu_custom_call" | custom-call | tf_op jit(solution)/shard_map/pallas_call | solution.py:634

commit v6 on v5

--- a/solution.py
+++ b/solution.py
@@ -225,10 +225,14 @@
     def g_pair(d):
         first = y_at(d) * TILES
         mine = grad[pl.ds(core * (HALF // 16) + first, TILES)].astype(jnp.float32)
-        return mine + g_core[pl.ds(first, TILES)].astype(jnp.float32)
+        theirs = g_core[pl.ds(first, TILES)].astype(jnp.float32)
+        soft = mine[:, 0] * jnp.exp(peak - near_peak) + theirs[:, 0] * jnp.exp(sibling_peak - near_peak)
+        return soft, mine[:, 1] + theirs[:, 1]
 
     def g_go(d):
-        g_send[d] = g_pair(d).astype(jnp.bfloat16)
+        soft, rows = g_pair(d)
+        g_send[d, :, 0] = soft.astype(jnp.bfloat16)
+        g_send[d, :, 1] = rows.astype(jnp.bfloat16)
         g_y_copy(d).start()
 
     loop(1, NEAR, lambda d: near_copy(d).start())
@@ -239,6 +243,11 @@
     minus = jnp.where(owned, -1.0, 0.0).astype(jnp.bfloat16)
     both = jnp.concatenate([raised.astype(jnp.bfloat16), minus], axis=1)
     sides[...] = jnp.dot(pt[...], both, preferred_element_type=jnp.float32)
+
+    tiles = (D // 16, 16, Q_DEV)
+    grad[:, 0] = sides[:, :Q_DEV].astype(jnp.bfloat16).reshape(tiles)
+    grad[:, 1] = sides[:, Q_DEV:].astype(jnp.bfloat16).reshape(tiles)
+    g_core_copy().start()
     pgt[...] = lax.dot_general(qt[...], minus, NT, preferred_element_type=jnp.float32)
     word = lax.broadcasted_iota(jnp.int32, (K, SLOT_DEV), 0).astype(jnp.float32)
     word = word.astype(jnp.bfloat16)
@@ -249,17 +258,12 @@
     loop(0, nz - 1, lambda e: far_copy(e).start())
     far[z] = mid[...]
 
-    tiles = (D // 16, 16, Q_DEV)
-    soft = sides[:, :Q_DEV] * jnp.exp(peak - near_peak)
-    grad[:, 0] = soft.astype(jnp.bfloat16).reshape(tiles)
-    grad[:, 1] = sides[:, Q_DEV:].astype(jnp.bfloat16).reshape(tiles)
-    g_core_copy().start()
+    sibling_peak = near[y * 2 + other, 0:1, :]
+    g_core_copy().wait_recv()
+    loop(1, NY, g_go)
     loop(1, NX, lambda d: q_copy(d).start())
     q_all[x] = qint[pl.ds(pl.multiple_of(x * HEAD_ROWS, 16), HEAD_ROWS), :]
-    onto_range(20, 28)
-    g_core_copy().wait_recv()
-    loop(1, NY, g_go)
-    onto_range(28, 72)
+    onto_range(20, 60)
 
     def g_part(t):
         return (pl.ds(t * G_TILE, G_TILE), slice(None))
@@ -285,10 +289,12 @@
         return copy(g_red.at[g_place(t)], g_final.at[g_part(t)], gr_send.at[g_place(t), e], gr_recv.at[t], to)
 
     loop(1, NY, lambda d: g_y_copy(d).wait_recv())
-    g_total = g_pair(0)
+    soft, rows = g_pair(0)
     for d in range(1, NY):
-        g_total = g_total + g_block[d].astype(jnp.float32)
-    g_sum[...] = g_total.astype(jnp.bfloat16)
+        soft = soft + g_block[d, :, 0].astype(jnp.float32)
+        rows = rows + g_block[d, :, 1].astype(jnp.float32)
+    g_sum[:, 0] = soft.astype(jnp.bfloat16)
+    g_sum[:, 1] = rows.astype(jnp.bfloat16)
     for t in range(TILES):
 
         @pl.when(z == g_owner(t))
@@ -299,7 +305,7 @@
         def _(t=t):
             z_copy(t).start()
 
-    onto_range(72, M)
+    onto_range(60, M)
     loop(0, nz - 1, lambda e: far_copy(e).wait_recv())
     last_peak, total, positive = merge(far[...])
     log_total = last_peak + jnp.log(total)

time: 61 us -> 60.6 us (level)
  no operation moved by 1% of the time
where the time goes in v6:
time: 60.6 us; the launch traced here: 60.5 us
  Pallas kernels  59.2 us (98%)
  between operations  1.29 us (2%)
    pallas_call x1, Pallas kernels, step(): pl.pallas_call(functools.partial(step_kernel, nz), out_shape=[pltpu.VMEM(...  58.1 us

profile of v6, /device:TPU:1, one launch (start us, length us, event | category | flops | bytes accessed | tf_op | source)
XLA Modules:
  0.0 60.5 jit_solution(12600869607148084686)
XLA Ops:
  1.3 58.1 %shard_map.85 = (f32[1,128]{1,0:T(1,128)S(1)}, f32[192,768]{1,0:T(8,128)S(1)}, f32[96,2048]{1,0:T(8,128)S(1)}) custom-call(s32[1]{0:T(128)S(6)} %copy.9.length_ref, s32[1,128]{1,0:T(1,128)} %bitcast.4, bf16[128,768]{1,0:T(8,128)(2,1)} %qin_hbm.1, bf16[768,768]{1,0:T(8,128)(2,1)} %weight_hbm.1, bf16[96,2048]{1,0:T(8,128)(2,1)} %codebook_hbm.1, s32[96,384]{1,0:T(8,128)} %bitcast.3), custom_call_target="tpu_custom_call" | custom-call | tf_op jit(solution)/shard_map/pallas_call | solution.py:577
  59.3 1.1 %shard_map.86 = (f32[1,128]{1,0:T(1,128)}, f32[192,768]{1,0:T(8,128)}, f32[96,2048]{1,0:T(8,128)}) custom-call(f32[1,128]{1,0:T(1,128)S(1)} %get-tuple-element.9.loss_in, f32[192,768]{1,0:T(8,128)S(1)} %get-tuple-element.10.head_in, f32[96,2048]{1,0:T(8,128)S(1)} %get-tuple-element.11.book_in), custom_call_target="tpu_custom_call" | custom-call | tf_op jit(solution)/shard_map/pallas_call | solution.py:640
